TPU v7x, 512 devices: a whole 4x4x16 slice. The times are simulated.
512 devices in a mesh: grp: 4 (over x), row: 16 (over y, z_hi), col: 8 (over z_lo, core).
Axes of the slice: x: 4, y: 4, z: 16 (z_hi: 4, z_lo: 4; z = z_hi * 4 + z_lo), core: 2. Of those that a mesh axis runs over, the one named last changes fastest.
Arguments:
- physical_values: bfloat16 [512, 100, 2688], P(('grp', 'row', 'col')), may hold values from -6 to 6
- samples_per_parallel: int32 [512], replicated, may hold values from 20 to 2688, as said below
- associated_polynomials: bfloat16 [640, 512, 640], P(('row', 'col'), 'grp'), may hold values from -4 to 4
- heat_salt_anomalies: float32 [2, 8, 256, 1024], P(None, None, ('grp', 'row'), 'col'), may hold values from -6 to 6
- courant_numbers: float32 [2, 8, 256, 1024], P(None, None, ('grp', 'row'), 'col'), may hold values from -0.35 to 0.35
- water_indicator: int32 [256, 1024], P(('grp', 'row'), 'col'), may hold values 0 or 1
- air_to_sea_coefficients: bfloat16 [256, 2, 1024, 128], P(('grp', 'row'), None, 'col'), may hold values from -0.375 to 0.375
- air_partner_span: int32 [256, 8, 2], P(('grp', 'row'), 'col'), may hold values from 0 to 167
- sea_to_air_coefficients: bfloat16 [512, 21, 128, 128], P(('grp', 'row', 'col')), may hold values from -0.5 to 0.5
- sea_partner_span: int32 [512, 21], P(('grp', 'row', 'col')), may hold values from 0 to 31
Outputs:
- spectral: bfloat16 [100, 2, 640, 640], P(None, None, ('row', 'col'), 'grp')
- tracers_out: float32 [2, 8, 256, 1024], P(None, None, ('grp', 'row'), 'col')
Inputs may be any that keep to these rules, and one draw needn't show every extreme that they name: `samples_per_parallel`: a multiple of 4; some row has exactly 2688 points.
All inputs are finite; a program needn't handle non-finite values. No bound on the sum of `water_indicator` on one device may be relied on, other than what follows from the above.
Results may differ from a plain program's by a relative error of at most 0.013.
Values may be sent and summed in bfloat16 or wider, within the bound.
A program may use at most 64 MiB of HBM per device.

v0:
```python
import math

import jax
import jax.numpy as jnp
from jax import lax
from jax.sharding import PartitionSpec as P

LEV = 10
REGRID_SPAN = 128
KSRC = 2
TSTEPS = 2


DIFFUSION = 0.07
COUPLE = 0.5
BLOCK_POINTS = 512


def extended(cells, sides, width):
    for axis, dim in sides:
        count = lax.axis_size(axis)
        ends = count - 1
        head = lax.slice_in_dim(cells, 0, width, axis=dim)
        tail = lax.slice_in_dim(cells, cells.shape[dim] - width, cells.shape[dim], axis=dim)
        cells = jnp.concatenate(
            [
                lax.ppermute(tail, axis, [(i, (i + 1) % count) for i in range(ends)]),
                cells,
                lax.ppermute(head, axis, [((i + 1) % count, i) for i in range(ends)]),
            ],
            axis=dim,
        )
    return cells


def fourier_table(block_start, point_count, orders):
    wave_count = orders.shape[1]
    places = block_start + lax.broadcasted_iota(jnp.int32, (BLOCK_POINTS, wave_count), 0)
    phase_index = places * orders % point_count
    angles = phase_index.astype(jnp.float32) * (2.0 * math.pi) / point_count.astype(jnp.float32)
    return jnp.concatenate([jnp.cos(angles), -jnp.sin(angles)], axis=1).astype(jnp.bfloat16)


def fourier_part(padded_row, point_count, orders):
    plane_count = padded_row.shape[0]
    wave_count = orders.shape[1]
    block_total = (point_count + BLOCK_POINTS - 1) // BLOCK_POINTS

    def add_block(block_index, running):
        block_start = (block_index * BLOCK_POINTS).astype(jnp.int32)
        segment = lax.dynamic_slice_in_dim(padded_row, block_start, BLOCK_POINTS, 1)
        places = block_start + lax.broadcasted_iota(jnp.int32, (1, BLOCK_POINTS), 1)
        segment = jnp.where(places < point_count, segment, jnp.zeros_like(segment))
        wave_table = fourier_table(block_start, point_count, orders)
        return running + jnp.dot(segment, wave_table, preferred_element_type=jnp.float32)

    return lax.fori_loop(
        0, block_total, add_block, jnp.zeros((plane_count, 2 * wave_count), jnp.float32)
    )


def finish(running, point_count, orders):
    plane_count = running.shape[0]
    wave_count = orders.shape[1]
    scaled = (running / point_count.astype(jnp.float32)).reshape(plane_count, 2, wave_count)
    wave_ids = orders.reshape(1, 1, wave_count)
    return jnp.where(2 * wave_ids < point_count, scaled, jnp.zeros_like(scaled)).astype(
        jnp.bfloat16
    )


def advance(tracer_ext, static_ext, levels):
    span_x = tracer_ext.shape[1]
    span_y = tracer_ext.shape[2]
    tracer_all = tracer_ext.reshape(2, levels, span_x, span_y)
    eastward = static_ext[:levels]
    northward = static_ext[levels : 2 * levels]
    wet_cells = static_ext[2 * levels]
    forcing = static_ext[2 * levels + 1 : 2 * levels + 3]
    pair_x = wet_cells[:-1, :] * wet_cells[1:, :]
    lower_x = tracer_all[:, :, :-1, :]
    upper_x = tracer_all[:, :, 1:, :]
    speed_x = eastward[:, :-1, :]
    flow_x = pair_x * (
        jnp.maximum(speed_x, 0.0) * lower_x
        + jnp.minimum(speed_x, 0.0) * upper_x
        - DIFFUSION * (upper_x - lower_x)
    )
    pair_y = wet_cells[:, :-1] * wet_cells[:, 1:]
    lower_y = tracer_all[:, :, :, :-1]
    upper_y = tracer_all[:, :, :, 1:]
    speed_y = northward[:, :, :-1]
    flow_y = pair_y * (
        jnp.maximum(speed_y, 0.0) * lower_y
        + jnp.minimum(speed_y, 0.0) * upper_y
        - DIFFUSION * (upper_y - lower_y)
    )
    spread = (
        flow_x[:, :, 1:, 1:-1]
        - flow_x[:, :, :-1, 1:-1]
        + flow_y[:, :, 1:-1, 1:]
        - flow_y[:, :, 1:-1, :-1]
    )
    push = COUPLE * forcing[:, 1:-1, 1:-1]
    source_levels = jnp.concatenate(
        [push[:, None], jnp.zeros((2, levels - 1, span_x - 2, span_y - 2), push.dtype)], axis=1
    )
    updated = tracer_all[:, :, 1:-1, 1:-1] + wet_cells[1:-1, 1:-1] * (source_levels - spread)
    return updated.reshape(2 * levels, span_x - 2, span_y - 2)


def local(
    physical_values,
    samples_per_parallel,
    associated_polynomials,
    heat_salt_anomalies,
    courant_numbers,
    water_indicator,
    air_to_sea_coefficients,
    air_partner_span,
    sea_to_air_coefficients,
    sea_partner_span,
):
    row_count = lax.axis_size("row")
    col_count = lax.axis_size("col")
    col_index = lax.axis_index("col")
    own_index = (lax.axis_index("grp") * row_count + lax.axis_index("row")) * col_count + col_index
    own_points = samples_per_parallel[own_index]
    parallel_samples = physical_values[0]
    plane_count, width = parallel_samples.shape
    local_waves = associated_polynomials.shape[0]
    wave_count = local_waves * row_count * col_count
    block_count = width // REGRID_SPAN
    positions = lax.broadcasted_iota(jnp.int32, (1, width), 1)
    flux_planes = jnp.stack([parallel_samples[LEV], parallel_samples[2 * LEV]])
    flux_planes = jnp.where(positions < own_points, flux_planes, jnp.zeros_like(flux_planes))
    flux_band = lax.all_gather(
        flux_planes.reshape(2, block_count, REGRID_SPAN), "col", axis=1, tiled=True
    )
    tile_rows = heat_salt_anomalies.shape[2]
    levels = heat_salt_anomalies.shape[1]
    picked = jnp.take(flux_band, air_partner_span.reshape(-1), axis=1).reshape(
        2, tile_rows, KSRC, REGRID_SPAN
    )
    forcing = jnp.einsum(
        "tkyj,qtkj->qty", air_to_sea_coefficients, picked, preferred_element_type=jnp.float32
    )
    ocean_state = heat_salt_anomalies.reshape(2 * levels, tile_rows, REGRID_SPAN)
    static = jnp.concatenate(
        [
            courant_numbers.reshape(2 * levels, tile_rows, REGRID_SPAN),
            water_indicator.astype(jnp.float32)[None],
            forcing,
        ]
    )
    static_ext = static
    for step_index in range(TSTEPS):
        outgoing = jnp.concatenate([ocean_state, static]) if step_index == 0 else ocean_state
        widened = extended(
            outgoing.astype(jnp.bfloat16), ((("grp", "row"), 1), ("col", 2)), 1
        ).astype(outgoing.dtype)
        if step_index == 0:
            static_ext = widened[2 * levels :]
        ocean_state = advance(widened[: 2 * levels], static_ext, levels)
    lowest_level_quantity = ocean_state[0].astype(jnp.bfloat16)
    sea_warmth_stretch = lax.all_gather(lowest_level_quantity, "col", axis=0, tiled=True)
    sea_warmth_selected = jnp.take(sea_warmth_stretch, sea_partner_span[0], axis=0)
    sea_warmth_samples = jnp.einsum(
        "vqy,vy->vq",
        sea_to_air_coefficients[0],
        sea_warmth_selected,
        preferred_element_type=jnp.float32,
    ).reshape(width)
    interface_heat_layer = (parallel_samples[0].astype(jnp.float32) + sea_warmth_samples).astype(
        jnp.bfloat16
    )
    lowest_level_parallel = jnp.concatenate([interface_heat_layer[None], parallel_samples[1:]])
    padded_row = jnp.pad(lowest_level_parallel, ((0, 0), (0, BLOCK_POINTS)))
    all_orders = lax.broadcasted_iota(jnp.int32, (1, wave_count), 1)
    running = fourier_part(padded_row, own_points, all_orders)
    coefficients = finish(running, own_points, all_orders)[None]
    arrived = lax.all_to_all(coefficients, ("row", "col"), split_axis=3, concat_axis=0, tiled=True)
    partial_value = jnp.einsum(
        "lfcm,mln->fcmn", arrived, associated_polynomials, preferred_element_type=jnp.float32
    )
    spectral = lax.psum_scatter(
        partial_value.astype(jnp.bfloat16), "grp", scatter_dimension=3, tiled=True
    )
    return (spectral, ocean_state.reshape(2, levels, tile_rows, REGRID_SPAN))


def solution(mesh):
    placed = (
        P(("grp", "row", "col"), None, None),
        P(),
        P(("row", "col"), "grp", None),
        P(None, None, ("grp", "row"), "col"),
        P(None, None, ("grp", "row"), "col"),
        P(("grp", "row"), "col"),
        P(("grp", "row"), None, "col", None),
        P(("grp", "row"), "col", None),
        P(("grp", "row", "col"), None, None, None),
        P(("grp", "row", "col"), None),
    )
    return jax.shard_map(
        local,
        mesh=mesh,
        in_specs=placed,
        out_specs=(P(None, None, ("row", "col"), "grp"), P(None, None, ("grp", "row"), "col")),
        check_vma=False,
    )
```

profile of v0, /device:TPU:1, one launch (start us, length us, event | category | flops | bytes accessed | tf_op | source)
XLA Modules:
  0.0 324.4 jit_solution(5502659596451704620)
XLA Ops:
  7.2 0.8 copy.47
  8.1 0.7 compare_and_fusion
  8.8 1.2 dynamic_slice.8
  10.0 0.6 add_compare_fusion
  10.5 0.8 slice_bitcast_fusion.2
  11.4 20.7 %all_gather.6 = bf16[2,168,128]{2,0,1:T(2,128)(2,1)S(1)} all-gather(bf16[2,21,128]{2,0,1:T(2,128)(2,1)S(1)} %broadcast_select_fusion), channel_id=1, replica_groups=mesh['grp'=4,'row'=16,'col'=8] {'col'}, dimensions={1}, use_global_device_ids=true | all-gather | bytes 96768 | tf_op jit(solution)/shard_map/all_gather | solution.py:137
  32.1 0.1 reshape.202
  32.2 0.1 copy.46
  32.3 0.6 gather_fusion
  32.9 1.2 fusion.24
  34.0 0.8 convert.27
  34.8 0.8 convert.28
  35.6 0.7 fusion.40
  36.3 4.3 %collective-permute-start = (bf16[35,1,128]{2,1,0:T(2,128)(2,1)S(1)}, bf16[35,1,128]{2,1,0:T(2,128)(2,1)S(1)}, u32[]{:S(2)}, u32[]{:S(2)}) collective-permute-start(bf16[35,1,128]{2,1,0:T(2,128)(2,1)S(1)} %get-tuple-element.148), channel_id=1, source_target_pairs={{0,8},{8,16},{16,24},{24,32},{32,40},{40,48},{48,56},{56,64},{64,7... | collective-permute-start | bytes 26888 | tf_op jit(solution)/shard_map/ppermute | solution.py:27
  40.7 1.3 collective-permute-start.1
  42.0 1.2 slice_bitcast_fusion
  43.2 6.7 %collective-permute-done.1 = bf16[35,1,128]{2,1,0:T(2,128)(2,1)S(1)} collective-permute-done((bf16[35,1,128]{2,1,0:T(2,128)(2,1)S(1)}, bf16[35,1,128]{2,1,0:T(2,128)(2,1)S(1)}, u32[]{:S(2)}, u32[]{:S(2)}) %collective-permute-start.1) | collective-permute-done | bytes 8992 | tf_op jit(solution)/shard_map/ppermute | solution.py:29
  50.0 0.1 fusion.47
  50.1 4.2 %collective-permute-start.2 = (bf16[35,6,1]{2,1,0:T(8,128)(2,1)S(1)}, bf16[35,6,1]{2,1,0:T(8,128)(2,1)S(1)}, u32[]{:S(2)}, u32[]{:S(2)}) collective-permute-start(bf16[35,6,1]{2,1,0:T(8,128)(2,1)S(1)} %get-tuple-element.146), channel_id=1, source_target_pairs={{0,1},{1,2},{2,3},{3,4},{4,5},{5,6},{6,7},{8,9},{9,10},{10,11},{11... | collective-permute-start | bytes 1268 | tf_op jit(solution)/shard_map/ppermute | solution.py:27
  54.3 1.9 collective-permute-start.3
  56.3 3.7 %collective-permute-done.3 = bf16[35,6,1]{2,1,0:T(8,128)(2,1)S(1)} collective-permute-done((bf16[35,6,1]{2,1,0:T(8,128)(2,1)S(1)}, bf16[35,6,1]{2,1,0:T(8,128)(2,1)S(1)}, u32[]{:S(2)}, u32[]{:S(2)}) %collective-permute-start.3) | collective-permute-done | bytes 452 | tf_op jit(solution)/shard_map/ppermute | solution.py:29
  60.0 0.3 maximum_convert_fusion
  60.6 0.1 subtract_multiply_fusion.2
  60.7 0.1 fusion.32
  60.9 6.1 %collective-permute-start.4 = (bf16[16,1,128]{2,0,1:T(8,128)(2,1)S(1)}, bf16[16,1,128]{2,0,1:T(8,128)(2,1)S(1)}, u32[]{:S(2)}, u32[]{:S(2)}) collective-permute-start(bf16[16,1,128]{2,0,1:T(8,128)(2,1)S(1)} %get-tuple-element.154), channel_id=1, source_target_pairs={{0,8},{8,16},{16,24},{24,32},{32,40},{40,48},{48,56},{56,64},{64,7... | collective-permute-start | bytes 12296 | tf_op jit(solution)/shard_map/ppermute | solution.py:27
  67.0 1.3 collective-permute-start.5
  68.3 0.6 multiply_compare_fusion
  71.1 4.2 %collective-permute-done.5 = bf16[16,1,128]{2,0,1:T(8,128)(2,1)S(1)} collective-permute-done((bf16[16,1,128]{2,0,1:T(8,128)(2,1)S(1)}, bf16[16,1,128]{2,0,1:T(8,128)(2,1)S(1)}, u32[]{:S(2)}, u32[]{:S(2)}) %collective-permute-start.5) | collective-permute-done | bytes 4128 | tf_op jit(solution)/shard_map/ppermute | solution.py:29
  75.3 0.1 fusion.49
  75.4 3.3 %collective-permute-start.6 = (bf16[16,6,1]{2,0,1:T(8,128)(2,1)S(1)}, bf16[16,6,1]{2,0,1:T(8,128)(2,1)S(1)}, u32[]{:S(2)}, u32[]{:S(2)}) collective-permute-start(bf16[16,6,1]{2,0,1:T(8,128)(2,1)S(1)} %get-tuple-element.150), channel_id=1, source_target_pairs={{0,1},{1,2},{2,3},{3,4},{4,5},{5,6},{6,7},{8,9},{9,10},{10,11},{11... | collective-permute-start | bytes 584 | tf_op jit(solution)/shard_map/ppermute | solution.py:27
  78.7 1.9 collective-permute-start.7
  80.6 0.1 reduce
  80.7 0.1 concatenate.42
  80.8 0.2 copy.50
  81.0 2.8 collective-permute-done.7
  83.8 0.1 reduce.1
  83.9 0.1 concatenate.44
  84.0 0.2 copy.52
  84.2 0.1 maximum_convert_fusion.1
  84.3 0.1 subtract_multiply_fusion
  84.4 0.8 fusion.45
  85.2 11.2 %all-gather = bf16[1,32,128]{2,0,1:T(2,128)(2,1)S(1)} all-gather(bf16[1,4,128]{2,0,1:T(2,128)(2,1)S(1)} %slice.239), channel_id=2, replica_groups=mesh['grp'=4,'row'=16,'col'=8] {'col'}, dimensions={1}, use_global_device_ids=true | all-gather | bytes 9216 | tf_op jit(solution)/shard_map/all_gather | solution.py:166
  96.4 0.6 gather_fusion.1
  97.0 0.1 select_bitcast_fusion
  97.0 0.5 fusion.26
  97.5 0.8 fusion.35
  98.3 0.1 fusion.28
  98.5 38.7 %while.13 = (s32[]{:T(128)}, f32[100,1280]{1,0:T(8,128)S(1)}, s32[]{:T(128)}, s32[]{:T(128)}, bf16[100,3200]{1,0:T(8,128)(2,1)S(1)}, /*index=5*/s32[]{:T(128)}, ...) while((s32[]{:T(128)}, f32[100,1280]{1,0:T(8,128)S(1)}, ...), condition=%wide.region_1.2_spmd.clone, body=%wide.region_0.1_spmd.clone.sunk | while | flops 138461696 | bytes 3777724 | solution.py:57
  98.6 18.4 %cosine_convert_fusion.2 = (bf16[512,640]{1,0:T(8,128)(2,1)S(1)}, bf16[512,640]{1,0:T(8,128)(2,1)S(1)}) fusion(f32[]{:T(128)} %get-tuple-element.241, pred[]{:T(512)} %get-tuple-element.240, s32[]{:T(128)} %get-tuple-element.239, s32[512]{0:T(512)S(1)} %iota_add_fusion.2), kind=kLoop, calls=%fused_computation.16.clone.1 | loop fusion | flops 4587520 | bytes 1312777 | tf_op jit(solution)/shard_map/convert
  117.0 0.6 broadcast_compare_fusion.2
  117.5 0.4 convolution_add_fusion.2
  117.9 18.4 %cosine_convert_fusion.2 = (bf16[512,640]{1,0:T(8,128)(2,1)S(1)}, bf16[512,640]{1,0:T(8,128)(2,1)S(1)}) fusion(f32[]{:T(128)} %get-tuple-element.241, pred[]{:T(512)} %get-tuple-element.240, s32[]{:T(128)} %get-tuple-element.239, s32[512]{0:T(512)S(1)} %iota_add_fusion.2), kind=kLoop, calls=%fused_computation.16.clone.1 | loop fusion | flops 4587520 | bytes 1312777 | tf_op jit(solution)/shard_map/convert
  136.3 0.6 broadcast_compare_fusion.2
  136.9 0.4 convolution_add_fusion.2
  137.4 0.2 select_convert_fusion
  137.6 1.0 copy.54
  138.6 110.6 %all_to_all.18 = bf16[1,100,2,640]{1,2,0,3:T(2,128)(2,1)S(1)} all-to-all(bf16[1,100,2,640]{1,2,0,3:T(2,128)(2,1)S(1)} %copy.54), channel_id=1, replica_groups=mesh['grp'=4,'row'=16,'col'=8] {'row','col'}, dimensions={3} | all-to-all | bytes 512000 | tf_op jit(solution)/shard_map/all_to_all | solution.py:182
  249.2 0.9 copy.55
  250.2 0.6 fusion.20
  250.7 5.6 %copy.56 = bf16[100,2,5,640]{0,1,2,3:T(2,128)(2,1)} copy(bf16[100,2,5,640]{3,0,1,2:T(8,128)(2,1)S(1)} %fusion.20) | data formatting | bytes 2560000 | tf_op jit(solution)/shard_map/convert_element_type | solution.py:187
  256.3 1.3 dynamic-slice
  258.3 57.2 %all-reduce.5.cloned.1.call-done = bf16[100,2,5,640]{0,1,2,3:T(2,128)(2,1)} async-done(((bf16[100,2,5,640]{0,1,2,3:T(2,128)(2,1)}), bf16[100,2,5,640]{0,1,2,3:T(2,128)(2,1)}) %all-reduce.5.cloned.1.call-update) | async-done | bytes 1280016
  315.5 1.3 constant_dynamic-slice_fusion
  316.7 0.8 copy.57
  (45 shorter events, 0.8 us)
Async XLA Ops:
  7.2 243.0 %copy-start = (bf16[5,128,640]{2,1,0:T(8,128)(2,1)S(1)}, bf16[5,128,640]{2,1,0:T(8,128)(2,1)}, u32[]{:S(2)}) copy-start(bf16[5,128,640]{2,1,0:T(8,128)(2,1)} %param.14) | copy-start | bytes 2457604
  7.2 36.0 %copy-start.2 = (s32[1,21]{1,0:T(1,128)S(1)}, s32[1,21]{1,0:T(1,128)}, u32[]{:S(2)}) copy-start(s32[1,21]{1,0:T(1,128)} %param.21) | copy-start | bytes 256
  7.2 308.3 %all-reduce.5.cloned.1.call-start = ((), (), s32[]{:S(2)}) async-start(), calls=%async_computation.1 | async-start | bytes 3276800
  36.3 6.9 %collective-permute-start = (bf16[35,1,128]{2,1,0:T(2,128)(2,1)S(1)}, bf16[35,1,128]{2,1,0:T(2,128)(2,1)S(1)}, u32[]{:S(2)}, u32[]{:S(2)}) collective-permute-start(bf16[35,1,128]{2,1,0:T(2,128)(2,1)S(1)} %get-tuple-element.148), channel_id=1, source_target_pairs={{0,8},{8,16},{16,24},{24,32},{32,40},{40,48},{48,56},{56,64},{64,7... | collective-permute-start | bytes 26888 | tf_op jit(solution)/shard_map/ppermute | solution.py:27
  40.7 9.2 %collective-permute-start.1 = (bf16[35,1,128]{2,1,0:T(2,128)(2,1)S(1)}, bf16[35,1,128]{2,1,0:T(2,128)(2,1)S(1)}, u32[]{:S(2)}, u32[]{:S(2)}) collective-permute-start(bf16[35,1,128]{2,1,0:T(2,128)(2,1)S(1)} %get-tuple-element.149), channel_id=1, source_target_pairs={{8,0},{16,8},{24,16},{32,24},{40,32},{48,40},{56,48},{64,56},{72,6... | collective-permute-start | bytes 26888 | tf_op jit(solution)/shard_map/ppermute | solution.py:29
  50.1 6.2 %collective-permute-start.2 = (bf16[35,6,1]{2,1,0:T(8,128)(2,1)S(1)}, bf16[35,6,1]{2,1,0:T(8,128)(2,1)S(1)}, u32[]{:S(2)}, u32[]{:S(2)}) collective-permute-start(bf16[35,6,1]{2,1,0:T(8,128)(2,1)S(1)} %get-tuple-element.146), channel_id=1, source_target_pairs={{0,1},{1,2},{2,3},{3,4},{4,5},{5,6},{6,7},{8,9},{9,10},{10,11},{11... | collective-permute-start | bytes 1268 | tf_op jit(solution)/shard_map/ppermute | solution.py:27
  54.3 5.7 %collective-permute-start.3 = (bf16[35,6,1]{2,1,0:T(8,128)(2,1)S(1)}, bf16[35,6,1]{2,1,0:T(8,128)(2,1)S(1)}, u32[]{:S(2)}, u32[]{:S(2)}) collective-permute-start(bf16[35,6,1]{2,1,0:T(8,128)(2,1)S(1)} %get-tuple-element.147), channel_id=1, source_target_pairs={{1,0},{2,1},{3,2},{4,3},{5,4},{6,5},{7,6},{9,8},{10,9},{11,10},{12... | collective-permute-start | bytes 1268 | tf_op jit(solution)/shard_map/ppermute | solution.py:29
  60.6 36.4 %copy-start.1 = (bf16[1,21,128,128]{3,2,1,0:T(8,128)(2,1)S(1)}, bf16[1,21,128,128]{3,2,1,0:T(8,128)(2,1)}, u32[]{:S(2)}) copy-start(bf16[1,21,128,128]{3,2,1,0:T(8,128)(2,1)} %param.20) | copy-start | bytes 2064388
  60.9 10.2 %collective-permute-start.4 = (bf16[16,1,128]{2,0,1:T(8,128)(2,1)S(1)}, bf16[16,1,128]{2,0,1:T(8,128)(2,1)S(1)}, u32[]{:S(2)}, u32[]{:S(2)}) collective-permute-start(bf16[16,1,128]{2,0,1:T(8,128)(2,1)S(1)} %get-tuple-element.154), channel_id=1, source_target_pairs={{0,8},{8,16},{16,24},{24,32},{32,40},{40,48},{48,56},{56,64},{64,7... | collective-permute-start | bytes 12296 | tf_op jit(solution)/shard_map/ppermute | solution.py:27
  67.0 8.3 %collective-permute-start.5 = (bf16[16,1,128]{2,0,1:T(8,128)(2,1)S(1)}, bf16[16,1,128]{2,0,1:T(8,128)(2,1)S(1)}, u32[]{:S(2)}, u32[]{:S(2)}) collective-permute-start(bf16[16,1,128]{2,0,1:T(8,128)(2,1)S(1)} %get-tuple-element.155), channel_id=1, source_target_pairs={{8,0},{16,8},{24,16},{32,24},{40,32},{48,40},{56,48},{64,56},{72,6... | collective-permute-start | bytes 12296 | tf_op jit(solution)/shard_map/ppermute | solution.py:29
  75.4 5.2 %collective-permute-start.6 = (bf16[16,6,1]{2,0,1:T(8,128)(2,1)S(1)}, bf16[16,6,1]{2,0,1:T(8,128)(2,1)S(1)}, u32[]{:S(2)}, u32[]{:S(2)}) collective-permute-start(bf16[16,6,1]{2,0,1:T(8,128)(2,1)S(1)} %get-tuple-element.150), channel_id=1, source_target_pairs={{0,1},{1,2},{2,3},{3,4},{4,5},{5,6},{6,7},{8,9},{9,10},{10,11},{11... | collective-permute-start | bytes 584 | tf_op jit(solution)/shard_map/ppermute | solution.py:27
  78.7 5.1 %collective-permute-start.7 = (bf16[16,6,1]{2,0,1:T(8,128)(2,1)S(1)}, bf16[16,6,1]{2,0,1:T(8,128)(2,1)S(1)}, u32[]{:S(2)}, u32[]{:S(2)}) collective-permute-start(bf16[16,6,1]{2,0,1:T(8,128)(2,1)S(1)} %get-tuple-element.151), channel_id=1, source_target_pairs={{1,0},{2,1},{3,2},{4,3},{5,4},{6,5},{7,6},{9,8},{10,9},{11,10},{12... | collective-permute-start | bytes 584 | tf_op jit(solution)/shard_map/ppermute | solution.py:29
Sparse Core Ops, SparseCore 0:
  256.4 58.9 all-reduce.4
where the time goes:
time: 325 us; the launch traced here: 324 us
  blocking collectives  142 us (44%)
  waiting for transfers between devices  74.7 us (23%)
  other arithmetic  45.3 us (14%)
  starting transfers between devices  24.4 us (8%)
  between operations  17.3 us (5%)
  local copies, waits for them, and re-layouts  17.2 us (5%)
    all_to_all x1, blocking collectives, local(): lax.all_to_all(coefficients, ('row', 'col'), split_axis=3, concat_axis=0,...  111 us
    unnamed x2, waiting for transfers between devices  57.2 us
    another operation x5, other arithmetic  39.1 us
    all_gather x1, blocking collectives, local(): lax.all_gather(flux_planes.reshape(2, block_count, REGRID_SPAN), 'col', a...  20.7 us
    ppermute x4, starting transfers between devices, extended(): lax.ppermute(tail, axis, [(i, (i + 1) % count) for i in range(ends)])  18 us
    ppermute x4, waiting for transfers between devices, extended(): lax.ppermute(head, axis, [((i + 1) % count, i) for i in range(ends)])  17.4 us
    all_gather x1, blocking collectives, local(): lax.all_gather(lowest_level_quantity, 'col', axis=0, tiled=True)  11.2 us
  transfers between devices with their start and end apart: 9, of which 5 were waited for; matrix products, arithmetic and copies ran while one was open for 1% of the time, Pallas kernels for 0%

commit v1 on v0

v1 whole, which is shorter than its diff:
```python
import math

import jax
import jax.numpy as jnp
from jax import lax
from jax.experimental import pallas as pl
from jax.experimental.pallas import tpu as pltpu
from jax.sharding import PartitionSpec as P

MESH = pl.DeviceIdType.MESH
F32 = jnp.float32
BF16 = jnp.bfloat16

NX, NY, NZ, NCORE = 4, 4, 16, 2
NROW, NCOL = 16, 8
CHIPS = NY * NZ

LEV = 10
PLANES = 100
POINTS = 2688
SPANS = 21
SPAN = 128
WAVES = 5
DEGREES = 160
LATS = 128
LINES = 4
TRACER_ROWS = 64
DIFFUSION = 0.07
COUPLE = 0.5

SEG = 256
SEGS = 11
PITCH = 112
PART = 25
PARTS = 4
PACKED = 8


def sincos(turns4):
    quarter = jnp.floor(turns4 + 0.5)
    y = (turns4 - quarter) * (0.5 * math.pi)
    y2 = y * y
    s = y * (1.0 + y2 * (-1.0 / 6 + y2 * (1.0 / 120 + y2 * (-1.0 / 5040 + y2 * (1.0 / 362880)))))
    c = 1.0 + y2 * (
        -0.5 + y2 * (1.0 / 24 + y2 * (-1.0 / 720 + y2 * (1.0 / 40320 + y2 * (-1.0 / 3628800))))
    )
    odd = (quarter == 1.0) | (quarter == 3.0)
    cos_sign = jnp.where((quarter == 1.0) | (quarter == 2.0), -1.0, 1.0)
    sin_sign = jnp.where((quarter == 2.0) | (quarter == 3.0), -1.0, 1.0)
    return cos_sign * jnp.where(odd, s, c), sin_sign * jnp.where(odd, c, s)


def dot_t(a, b):
    return lax.dot_general(a, b, (((1,), (1,)), ((), ())), preferred_element_type=F32)


def kernel(
    phys_hbm,
    poly_hbm,
    s2a_hbm,
    a2s_hbm,
    tracer_ref,
    courant_ref,
    water_ref,
    points_ref,
    air_ref,
    sea_ref,
    spectral_ref,
    tracer_out_ref,
    xv,
    pv,
    s2av,
    a2sv,
    x32,
    flux32,
    flux_got32,
    sst_got32,
    rows32,
    cells32,
    shifted,
    tops,
    bottoms,
    forced,
    table_c,
    table_s,
    waves,
    segments,
    product,
    fourier,
    row0,
    parts,
    packed32,
    out32,
    right_hand,
    got32,
    product2,
    poly_t,
    flux_send,
    flux_got,
    down_send,
    up_send,
    cells_send,
    top1,
    bottom1,
    left1,
    right1,
    down2_send,
    up2_send,
    cells2_send,
    top2,
    bottom2,
    left2,
    right2,
    sst_send,
    sst_got,
    poly_got,
    core_send,
    core_got,
    outbox,
    inbox,
    local_sem,
    flux_ss,
    flux_rs,
    halo_ss,
    halo_rs,
    halo2_ss,
    halo2_rs,
    sst_ss,
    sst_rs,
    poly_ss,
    poly_rs,
    core_ss,
    core_rs,
    all_ss,
    all_rs,
    ring_ss,
    ring_rs,
    ready,
):
    x = lax.axis_index("grp")
    row = lax.axis_index("row")
    col = lax.axis_index("col")
    y = row // 4
    z = lax.rem(row, 4) * 4 + col // 2
    core = lax.rem(col, 2)
    strip = x * NROW + row

    def at(xx, yy, zz, cc):
        return (xx, yy * 4 + zz // 4, lax.rem(zz, 4) * 2 + cc)

    def remote(src, dst, ss, rs, device):
        return pltpu.make_async_remote_copy(
            src_ref=src, dst_ref=dst, send_sem=ss, recv_sem=rs, device_id=device, device_id_type=MESH
        )

    def strip_at(other):
        return (other // NROW, lax.rem(other, NROW), col)

    below = strip_at(lax.rem(strip + 1, NX * NROW))
    above = strip_at(lax.rem(strip + NX * NROW - 1, NX * NROW))
    band = [(x, row, lax.rem(col + i, NCOL)) for i in range(1, NCOL)]
    after = band[0]
    before = band[-1]
    z_ring = [at(x, y, lax.rem(z + i, NZ), core) for i in range(1, NZ)]
    y_ring = [at(x, lax.rem(y + i, NY), z, core) for i in range(1, NY)]
    x_ring = [at(lax.rem(x + i, NX), y, z, core) for i in range(1, NX)]
    sibling = at(x, y, z, 1 - core)

    ins = [
        pltpu.make_async_copy(phys_hbm, xv, local_sem.at[0]),
        pltpu.make_async_copy(poly_hbm, pv, local_sem.at[1]),
        pltpu.make_async_copy(a2s_hbm, a2sv, local_sem.at[2]),
        pltpu.make_async_copy(s2a_hbm, s2av, local_sem.at[3]),
    ]
    for copy in ins:
        copy.start()
    barrier = pltpu.get_barrier_semaphore()
    greeted = band + [below, above, sibling] + x_ring + y_ring + z_ring
    for device in greeted:
        pl.semaphore_signal(barrier, inc=1, device_id=device, device_id_type=MESH)

    own = strip * NCOL + col
    n = points_ref[own]
    lane = lax.broadcasted_iota(jnp.int32, (1, SPAN), 1)

    ins[0].wait()
    x32[...] = xv[0, 0:32, :].astype(F32)
    flux32[...] = jnp.zeros_like(flux32)
    for b in range(SPANS):
        live = lane + b * SPAN < n
        for q in range(2):
            line = x32[(q + 1) * LEV : (q + 1) * LEV + 1, b * SPAN : (b + 1) * SPAN]
            flux32[q * 24 + b : q * 24 + b + 1, :] = jnp.where(live, line, 0.0)
    flux_send[...] = flux32[...].astype(BF16)
    flux_got[pl.ds(col, 1)] = flux_send[...][None]

    wet = water_ref[...].astype(F32)
    for i in range(16):
        cells32[96 + 4 * i : 100 + 4 * i, :] = wet
    cells32[0:64, :] = tracer_ref[...]
    cells32[64:96, :] = courant_ref[32:64, :]
    cells_send[...] = cells32[...].astype(BF16)
    rows32[...] = jnp.zeros_like(rows32)
    rows32[0:16, :] = tracer_ref[pl.ds(3, 16, stride=4), :]
    rows32[16:24, :] = courant_ref[pl.ds(3, 8, stride=4), :]
    rows32[24:25, :] = wet[3:4, :]
    down_send[...] = rows32[...].astype(BF16)
    rows32[0:16, :] = tracer_ref[pl.ds(0, 16, stride=4), :]
    rows32[24:25, :] = wet[0:1, :]
    up_send[...] = rows32[...].astype(BF16)

    pl.semaphore_wait(barrier, len(greeted))
    flux_copies = [
        remote(flux_send, flux_got.at[col], flux_ss.at[i], flux_rs.at[i], device)
        for i, device in enumerate(band)
    ]
    halo_copies = [
        remote(down_send, top1, halo_ss.at[0], halo_rs.at[0], below),
        remote(up_send, bottom1, halo_ss.at[1], halo_rs.at[1], above),
        remote(cells_send, left1, halo_ss.at[2], halo_rs.at[2], after),
        remote(cells_send, right1, halo_ss.at[3], halo_rs.at[3], before),
    ]
    for copy in flux_copies + halo_copies:
        copy.start()
    for device in y_ring:
        pl.semaphore_signal(ready, inc=1, device_id=device, device_id_type=MESH)

    shape = (WAVES, 48, SPAN)
    k_of = lax.broadcasted_iota(jnp.int32, shape, 0)
    p_row = lax.broadcasted_iota(jnp.int32, shape, 1)
    d_of = lax.broadcasted_iota(jnp.int32, shape, 2)
    owner = (d_of & 3) * 32 + ((d_of >> 2) & 15) * 2 + (d_of >> 6)
    orders = owner * WAVES + k_of
    places = jnp.where(
        p_row < 16, p_row, jnp.where(p_row < 32, (p_row - 16) * 16, (p_row - 32) * SEG)
    )
    count = jnp.full(shape, n, jnp.int32).astype(F32)
    inverse = 1.0 / count
    turns = orders.astype(F32) * places.astype(F32)
    phase = turns - jnp.floor(turns * inverse) * count
    phase = jnp.where(phase < 0.0, phase + count, phase)
    phase = jnp.where(phase >= count, phase - count, phase)
    cosine, sine = sincos(phase * (4.0 * inverse))
    table_c[...] = cosine
    table_s[...] = -sine

    def fill_waves(a, _):
        start = pl.multiple_of(a * 16, 16)
        for k in range(WAVES):
            ac = table_c[k, pl.ds(16 + a, 1), :]
            as_ = table_s[k, pl.ds(16 + a, 1), :]
            bc = table_c[k, 0:16, :]
            bs = table_s[k, 0:16, :]
            waves[k, pl.ds(start, 16), 0:SPAN] = (ac * bc - as_ * bs).astype(BF16)
            waves[k, pl.ds(start, 16), SPAN : 2 * SPAN] = (ac * bs + as_ * bc).astype(BF16)
        return 0

    lax.fori_loop(0, 16, fill_waves, 0)

    for i in range(SEGS):
        width = min(SEG, POINTS - i * SEG)
        pos = i * SEG + lax.broadcasted_iota(jnp.int32, (1, width), 1)
        values = xv[0, :, i * SEG : i * SEG + width].astype(F32)
        values = jnp.where(pos < n, values, 0.0).astype(BF16)
        segments[i * PITCH + 96 : (i + 1) * PITCH, :] = jnp.zeros((16, SEG), BF16)
        if width < SEG:
            segments[i * PITCH : (i + 1) * PITCH, width:SEG] = jnp.zeros((PITCH, SEG - width), BF16)
        segments[i * PITCH : i * PITCH + PLANES, 0:width] = values

    ins[1].wait()
    for k in range(WAVES):
        turned = pv[k].astype(F32).T.astype(BF16)
        for g in range(NX):
            poly_t[g, k * DEGREES : (k + 1) * DEGREES, :] = turned[g * DEGREES : (g + 1) * DEGREES]
    poly_got[0] = poly_t[x]
    poly_copies = [
        remote(
            poly_t.at[lax.rem(x + i, NX)],
            poly_got.at[i],
            poly_ss.at[i - 1],
            poly_rs.at[i - 1],
            x_ring[i - 1],
        )
        for i in range(1, NX)
    ]
    for copy in poly_copies:
        copy.start()

    ins[2].wait()
    for copy in flux_copies:
        copy.wait_recv()
    flux_got32[...] = flux_got[...].astype(F32)
    two = lax.broadcasted_iota(jnp.int32, (16, SPAN), 0)
    forced[...] = jnp.zeros_like(forced)
    for line in range(LINES):
        total = jnp.zeros((16, SPAN), F32)
        for k in range(2):
            span = air_ref[0, k, line]
            source = lax.div(span, SPANS)
            block = lax.rem(span, SPANS)
            first = flux_got32[source, pl.ds(block, 1), :]
            second = flux_got32[source, pl.ds(block + 24, 1), :]
            pair = jnp.where(
                two == 0, jnp.broadcast_to(first, (16, SPAN)), jnp.broadcast_to(second, (16, SPAN))
            )
            total = total + dot_t(pair.astype(BF16), a2sv[line, k])
        forced[line : line + 1, :] = COUPLE * total[0:1, :]
        forced[32 + line : 33 + line, :] = COUPLE * total[1:2, :]

    has_top = jnp.where(strip > 0, 1.0, 0.0).astype(F32)
    has_bottom = jnp.where(strip < NX * NROW - 1, 1.0, 0.0).astype(F32)
    has_left = jnp.where(col > 0, 1.0, 0.0).astype(F32)
    has_right = jnp.where(col < NCOL - 1, 1.0, 0.0).astype(F32)
    line_of = lax.broadcasted_iota(jnp.int32, (TRACER_ROWS, SPAN), 0) & 3
    lane_of = lax.broadcasted_iota(jnp.int32, (TRACER_ROWS, SPAN), 1)

    def from_above(value, edge):
        shifted[8:72, :] = value
        tops[pl.ds(0, 16, stride=4), :] = edge
        return jnp.where(line_of == 0, tops[...], shifted[7:71, :])

    def from_below(value, edge):
        shifted[8:72, :] = value
        bottoms[pl.ds(3, 16, stride=4), :] = edge
        return jnp.where(line_of == 3, bottoms[...], shifted[9:73, :])

    def from_left(value, tile):
        return jnp.where(lane_of == 0, pltpu.roll(tile, 1, 1), pltpu.roll(value, 1, 1))

    def from_right(value, tile):
        return jnp.where(
            lane_of == SPAN - 1, pltpu.roll(tile, SPAN - 1, 1), pltpu.roll(value, SPAN - 1, 1)
        )

    def twice(value):
        return jnp.concatenate([value, value], axis=0)

    for copy in halo_copies:
        copy.wait_recv()
    shifted[...] = jnp.zeros_like(shifted)
    tops[...] = jnp.zeros_like(tops)
    bottoms[...] = jnp.zeros_like(bottoms)
    top = top1[...].astype(F32) * has_top
    bottom = bottom1[...].astype(F32) * has_bottom
    left = left1[...].astype(F32) * has_left
    right = right1[...].astype(F32) * has_right
    wet64 = cells32[96:160, :]
    east = twice(courant_ref[0:32, :])
    north = twice(courant_ref[32:64, :])
    east_up = from_above(east, twice(top[16:24, :]))
    north_left = from_left(north, twice(left[64:96, :]))
    pair_up = wet64 * from_above(wet64, jnp.broadcast_to(top[24:25, :], (16, SPAN)))
    pair_down = wet64 * from_below(wet64, jnp.broadcast_to(bottom[24:25, :], (16, SPAN)))
    pair_left = wet64 * from_left(wet64, left[96:160, :])
    pair_right = wet64 * from_right(wet64, right[96:160, :])

    def flow(pair, speed, low, high):
        return pair * (
            jnp.maximum(speed, 0.0) * low
            + jnp.minimum(speed, 0.0) * high
            - DIFFUSION * (high - low)
        )

    def advance(q, edge_top, edge_bottom, tile_left, tile_right):
        spread = (
            flow(pair_down, east, q, from_below(q, edge_bottom))
            - flow(pair_up, east_up, from_above(q, edge_top), q)
            + flow(pair_right, north, q, from_right(q, tile_right))
            - flow(pair_left, north_left, from_left(q, tile_left), q)
        )
        return q + wet64 * (forced[...] - spread)

    state = advance(
        tracer_ref[...], top[0:16, :], bottom[0:16, :], left[0:64, :], right[0:64, :]
    )
    tracer_out_ref[...] = state
    cells2_send[...] = state.astype(BF16)
    down2_send[...] = tracer_out_ref[pl.ds(3, 16, stride=4), :].astype(BF16)
    up2_send[...] = tracer_out_ref[pl.ds(0, 16, stride=4), :].astype(BF16)
    halo2_copies = [
        remote(down2_send, top2, halo2_ss.at[0], halo2_rs.at[0], below),
        remote(up2_send, bottom2, halo2_ss.at[1], halo2_rs.at[1], above),
        remote(cells2_send, left2, halo2_ss.at[2], halo2_rs.at[2], after),
        remote(cells2_send, right2, halo2_ss.at[3], halo2_rs.at[3], before),
    ]
    for copy in halo2_copies:
        copy.start()

    inverse_row = 1.0 / jnp.full((1, SPAN), n, jnp.int32).astype(F32)
    d_row = lax.broadcasted_iota(jnp.int32, (1, SPAN), 1)
    owner_row = (d_row & 3) * 32 + ((d_row >> 2) & 15) * 2 + (d_row >> 6)

    def scale_of(k):
        return jnp.where(2 * (owner_row * WAVES + k) < n, inverse_row, 0.0)

    def transform(k, _):
        product[...] = jnp.dot(segments[...], waves[k], preferred_element_type=F32)
        real = jnp.zeros((PITCH, SPAN), F32)
        imag = jnp.zeros((PITCH, SPAN), F32)
        for i in range(SEGS):
            wc = table_c[k, 32 + i : 33 + i, :]
            ws = table_s[k, 32 + i : 33 + i, :]
            yc = product[i * PITCH : (i + 1) * PITCH, 0:SPAN]
            ys = product[i * PITCH : (i + 1) * PITCH, SPAN : 2 * SPAN]
            real = real + (yc * wc - ys * ws)
            imag = imag + (yc * ws + ys * wc)
        scale = scale_of(k)
        fourier[k, 0] = real * scale
        fourier[k, 1] = imag * scale
        return 0

    lax.fori_loop(0, 3, transform, 0)

    for copy in halo2_copies:
        copy.wait_recv()
    state = advance(
        tracer_out_ref[...],
        top2[...].astype(F32) * has_top,
        bottom2[...].astype(F32) * has_bottom,
        left2[...].astype(F32) * has_left,
        right2[...].astype(F32) * has_right,
    )
    tracer_out_ref[...] = state
    sst_send[...] = state[0:16, :].astype(BF16)
    sst_got[pl.ds(col, 1)] = sst_send[...][None]
    sst_copies = [
        remote(sst_send, sst_got.at[col], sst_ss.at[i], sst_rs.at[i], device)
        for i, device in enumerate(band)
    ]
    for copy in sst_copies:
        copy.start()

    lax.fori_loop(3, WAVES, transform, 0)

    ins[3].wait()
    for copy in sst_copies:
        copy.wait_recv()
    sst_got32[...] = sst_got[...].astype(F32)
    row0[...] = jnp.zeros_like(row0)
    for b in range(SPANS):
        span = sea_ref[0, b]
        source = lax.div(span, LINES)
        line = lax.rem(span, LINES)
        warmth = jnp.broadcast_to(sst_got32[source, pl.ds(line, 1), :], (16, SPAN))
        sampled = dot_t(warmth.astype(BF16), s2av[0, b])[0:1, :]
        plane = x32[0:1, b * SPAN : (b + 1) * SPAN] + sampled
        plane = jnp.where(lane + b * SPAN < n, plane, 0.0)
        half = (b % 2) * SPAN
        row0[b // 2 : b // 2 + 1, half : half + SPAN] = plane
    surface = row0[...].astype(BF16)
    for k in range(WAVES):
        part = jnp.dot(surface, waves[k], preferred_element_type=F32)
        wc = table_c[k, 32:48, :]
        ws = table_s[k, 32:48, :]
        yc = part[:, 0:SPAN]
        ys = part[:, SPAN : 2 * SPAN]
        scale = scale_of(k)
        fourier[k, 0, 0:1, :] = jnp.sum(yc * wc - ys * ws, axis=0, keepdims=True) * scale
        fourier[k, 1, 0:1, :] = jnp.sum(yc * ws + ys * wc, axis=0, keepdims=True) * scale

    for c in range(2):
        for q in range(PARTS):
            r = c * PARTS + q
            parts[r, 120:128, :] = jnp.zeros((8, SPAN), F32)
            for k in range(WAVES):
                parts[r, k * PART : (k + 1) * PART, :] = fourier[
                    k, c, q * PART : (q + 1) * PART, :
                ]
            packed32[pl.ds(r, LATS, stride=PACKED), :] = parts[r].T

    half_rows = CHIPS * PACKED
    core_send[...] = packed32[pl.ds(pl.multiple_of((1 - core) * half_rows, 8), half_rows), :].astype(
        BF16
    )
    core_copy = remote(core_send, core_got, core_ss, core_rs, sibling)
    core_copy.start()
    mine = packed32[pl.ds(pl.multiple_of(core * half_rows, 8), half_rows), :].reshape(
        CHIPS, PACKED, SPAN
    )
    core_copy.wait_recv()
    theirs = core_got[...].astype(F32).reshape(CHIPS, PACKED, SPAN)
    is_first = core == 0
    out32[:, 0:PACKED, :] = jnp.where(is_first, mine, theirs)
    out32[:, PACKED : 2 * PACKED, :] = jnp.where(is_first, theirs, mine)
    outbox[...] = out32[...].astype(BF16)
    pl.semaphore_wait(ready, NY - 1)
    me = y * NZ + z

    def post(i, _):
        zz = lax.rem(z + i, NZ)
        for j in range(NY):
            yy = lax.rem(y + j, NY)
            remote(
                outbox.at[zz * NY + yy], inbox.at[0, me], all_ss, all_rs, at(x, yy, zz, core)
            ).start()
        return 0

    lax.fori_loop(1, NZ, post, 0)
    for j in range(1, NY):
        yy = lax.rem(y + j, NY)
        remote(outbox.at[z * NY + yy], inbox.at[0, me], all_ss, all_rs, at(x, yy, z, core)).start()
    inbox[0, pl.ds(me, 1)] = outbox[pl.ds(z * NY + y, 1)]

    for copy in flux_copies + halo_copies + halo2_copies + sst_copies + poly_copies:
        copy.wait_send()
    core_copy.wait_send()
    for copy in poly_copies:
        copy.wait_recv()
    degrees = jnp.concatenate([poly_got[i] for i in range(NX)], axis=1)

    every = remote(
        outbox.at[pl.ds(0, CHIPS - 1)],
        inbox.at[0, pl.ds(0, CHIPS - 1)],
        all_ss,
        all_rs,
        sibling,
    )
    every.wait_recv()
    next_x = x_ring[0]
    last_x = x_ring[-1]
    ring_right = remote(inbox.at[0], inbox.at[1], ring_ss.at[0], ring_rs.at[0], next_x)
    ring_left = remote(inbox.at[0], inbox.at[3], ring_ss.at[1], ring_rs.at[1], last_x)
    ring_right.start()
    ring_left.start()

    def unpack(slot):
        got32[...] = inbox[slot].astype(F32).reshape(CHIPS * 2 * PACKED, SPAN)
        for r in range(PACKED):
            right_hand[slot * LATS : (slot + 1) * LATS, r * SPAN : (r + 1) * SPAN] = got32[
                pl.ds(r, LATS, stride=PACKED), :
            ].astype(BF16)

    unpack(0)
    middle = CHIPS // 2
    ring_right.wait_recv()
    on_right = remote(
        inbox.at[1, pl.ds(0, middle)],
        inbox.at[2, pl.ds(0, middle)],
        ring_ss.at[2],
        ring_rs.at[2],
        next_x,
    )
    on_right.start()
    ring_left.wait_recv()
    on_left = remote(
        inbox.at[3, pl.ds(middle, middle)],
        inbox.at[2, pl.ds(middle, middle)],
        ring_ss.at[3],
        ring_rs.at[3],
        last_x,
    )
    on_left.start()
    unpack(1)
    unpack(3)
    on_right.wait_recv()
    on_left.wait_recv()
    unpack(2)

    lanes = lax.broadcasted_iota(jnp.int32, (DEGREES, SPAN), 1)
    for c in range(2):
        for pair in range(2):
            start = (c * PARTS + pair * 2) * SPAN
            product2[:, pair * 2 * SPAN : (pair + 1) * 2 * SPAN] = jnp.dot(
                degrees, right_hand[:, start : start + 2 * SPAN], preferred_element_type=F32
            )
        for k in range(WAVES):
            total = jnp.zeros((DEGREES, SPAN), F32)
            for q in range(PARTS):
                block = product2[k * DEGREES : (k + 1) * DEGREES, q * SPAN : (q + 1) * SPAN]
                turn = (PART * (q - k)) % SPAN
                if turn:
                    block = pltpu.roll(block, turn, 1)
                keep = (lanes >= q * PART) & (lanes < (q + 1) * PART)
                total = jnp.where(keep, block, total)
            spectral_ref[c, k] = total[:, 0:PLANES].astype(BF16)

    every.wait_send()
    for copy in (ring_right, ring_left, on_right, on_left):
        copy.wait_send()


def local(
    physical_values,
    samples_per_parallel,
    associated_polynomials,
    heat_salt_anomalies,
    courant_numbers,
    water_indicator,
    air_to_sea_coefficients,
    air_partner_span,
    sea_to_air_coefficients,
    sea_partner_span,
):
    vmem = pl.BlockSpec(memory_space=pltpu.VMEM)
    smem = pl.BlockSpec(memory_space=pltpu.SMEM)
    anywhere = pl.BlockSpec(memory_space=pl.ANY)
    dma = pltpu.SemaphoreType.DMA
    scratch = [
        pltpu.VMEM((1, PLANES, POINTS), BF16),
        pltpu.VMEM((WAVES, LATS, NX * DEGREES), BF16),
        pltpu.VMEM((1, SPANS, SPAN, SPAN), BF16),
        pltpu.VMEM((LINES, 2, SPAN, SPAN), BF16),
        pltpu.VMEM((32, POINTS), F32),
        pltpu.VMEM((48, SPAN), F32),
        pltpu.VMEM((NCOL, 48, SPAN), F32),
        pltpu.VMEM((NCOL, 16, SPAN), F32),
        pltpu.VMEM((32, SPAN), F32),
        pltpu.VMEM((160, SPAN), F32),
        pltpu.VMEM((80, SPAN), F32),
        pltpu.VMEM((TRACER_ROWS, SPAN), F32),
        pltpu.VMEM((TRACER_ROWS, SPAN), F32),
        pltpu.VMEM((TRACER_ROWS, SPAN), F32),
        pltpu.VMEM((WAVES, 48, SPAN), F32),
        pltpu.VMEM((WAVES, 48, SPAN), F32),
        pltpu.VMEM((WAVES, SEG, 2 * SPAN), BF16),
        pltpu.VMEM((SEGS * PITCH, SEG), BF16),
        pltpu.VMEM((SEGS * PITCH, 2 * SPAN), F32),
        pltpu.VMEM((WAVES, 2, PITCH, SPAN), F32),
        pltpu.VMEM((16, SEG), F32),
        pltpu.VMEM((PACKED, SPAN, SPAN), F32),
        pltpu.VMEM((LATS * PACKED, SPAN), F32),
        pltpu.VMEM((CHIPS, 2 * PACKED, SPAN), F32),
        pltpu.VMEM((NX * LATS, PACKED * SPAN), BF16),
        pltpu.VMEM((LATS * PACKED, SPAN), F32),
        pltpu.VMEM((WAVES * DEGREES, PARTS * SPAN), F32),
        pltpu.VMEM((NX, WAVES * DEGREES, LATS), BF16),
        pltpu.VMEM((48, SPAN), BF16),
        pltpu.VMEM((NCOL, 48, SPAN), BF16),
        pltpu.VMEM((32, SPAN), BF16),
        pltpu.VMEM((32, SPAN), BF16),
        pltpu.VMEM((160, SPAN), BF16),
        pltpu.VMEM((32, SPAN), BF16),
        pltpu.VMEM((32, SPAN), BF16),
        pltpu.VMEM((160, SPAN), BF16),
        pltpu.VMEM((160, SPAN), BF16),
        pltpu.VMEM((16, SPAN), BF16),
        pltpu.VMEM((16, SPAN), BF16),
        pltpu.VMEM((64, SPAN), BF16),
        pltpu.VMEM((16, SPAN), BF16),
        pltpu.VMEM((16, SPAN), BF16),
        pltpu.VMEM((64, SPAN), BF16),
        pltpu.VMEM((64, SPAN), BF16),
        pltpu.VMEM((16, SPAN), BF16),
        pltpu.VMEM((NCOL, 16, SPAN), BF16),
        pltpu.VMEM((NX, WAVES * DEGREES, LATS), BF16),
        pltpu.VMEM((CHIPS * PACKED, SPAN), BF16),
        pltpu.VMEM((CHIPS * PACKED, SPAN), BF16),
        pltpu.VMEM((CHIPS, 2 * PACKED, SPAN), BF16),
        pltpu.VMEM((NX, CHIPS, 2 * PACKED, SPAN), BF16),
        dma((4,)),
        dma((NCOL - 1,)),
        dma((NCOL - 1,)),
        dma((4,)),
        dma((4,)),
        dma((4,)),
        dma((4,)),
        dma((NCOL - 1,)),
        dma((NCOL - 1,)),
        dma((NX - 1,)),
        dma((NX - 1,)),
        dma,
        dma,
        dma,
        dma,
        dma((4,)),
        dma((4,)),
        pltpu.SemaphoreType.REGULAR,
    ]
    spectral, tracers = pl.pallas_call(
        kernel,
        out_shape=(
            jax.ShapeDtypeStruct((2, WAVES, DEGREES, PLANES), BF16),
            jax.ShapeDtypeStruct((TRACER_ROWS, SPAN), F32),
        ),
        in_specs=[anywhere] * 4 + [vmem] * 3 + [smem] * 3,
        out_specs=(vmem, vmem),
        scratch_shapes=scratch,
        compiler_params=pltpu.CompilerParams(
            collective_id=0, has_side_effects=True, vmem_limit_bytes=48 * 2**20
        ),
        cost_estimate=pl.CostEstimate(
            flops=1_000_000_000, bytes_accessed=3_000_000, transcendentals=0
        ),
    )(
        physical_values,
        associated_polynomials,
        sea_to_air_coefficients,
        air_to_sea_coefficients,
        heat_salt_anomalies.reshape(TRACER_ROWS, SPAN),
        courant_numbers.reshape(TRACER_ROWS, SPAN),
        water_indicator,
        samples_per_parallel,
        jnp.transpose(air_partner_span, (1, 2, 0)),
        sea_partner_span,
    )
    return spectral.transpose(3, 0, 1, 2), tracers.reshape(2, 8, LINES, SPAN)


def solution(mesh):
    placed = (
        P(("grp", "row", "col"), None, None),
        P(),
        P(("row", "col"), "grp", None),
        P(None, None, ("grp", "row"), "col"),
        P(None, None, ("grp", "row"), "col"),
        P(("grp", "row"), "col"),
        P(("grp", "row"), None, "col", None),
        P(("grp", "row"), "col", None),
        P(("grp", "row", "col"), None, None, None),
        P(("grp", "row", "col"), None),
    )
    return jax.shard_map(
        local,
        mesh=mesh,
        in_specs=placed,
        out_specs=(P(None, None, ("row", "col"), "grp"), P(None, None, ("grp", "row"), "col")),
        check_vma=False,
    )
```

time: 325 us -> 76.2 us (0.23)
  the two profiles are of different devices: /device:TPU:1 before, /device:TPU:2 now
where the time goes in v1:
time: 76.2 us; the launch traced here: 75.7 us
  Pallas kernels  67.2 us (88%)
  local copies, waits for them, and re-layouts  7.81 us (10%)
    pallas_call x1, Pallas kernels, local(): pl.pallas_call(kernel, out_shape=(jax.ShapeDtypeStruct((2, WAVES, DEGREES...  67.2 us
    unnamed x22, local copies, waits for them, and re-layouts  7.81 us

profile of v1, /device:TPU:2, one launch (start us, length us, event | category | flops | bytes accessed | tf_op | source)
XLA Modules:
  0.0 75.7 jit_solution(5232746134965438414)
XLA Ops:
  0.6 0.0 copy-start.7
  0.6 0.0 copy-start.6
  0.7 0.0 copy-start.8
  0.7 0.0 copy-start.9
  0.7 0.6 copy-done.7
  1.3 0.0 copy-done.6
  1.3 0.0 copy-done.8
  1.3 0.0 copy-done.9
  1.3 0.0 copy-start
  1.4 1.1 %copy-done = bf16[5,128,640]{2,1,0:T(8,128)(2,1)S(1)} copy-done((bf16[5,128,640]{2,1,0:T(8,128)(2,1)S(1)}, bf16[5,128,640]{2,1,0:T(8,128)(2,1)}, u32[]{:S(2)}) %copy-start) | copy-done | bytes 819224
  2.5 0.0 copy-start.1
  2.5 1.1 %copy-done.1 = bf16[1,21,128,128]{3,2,1,0:T(8,128)(2,1)S(1)} copy-done((bf16[1,21,128,128]{3,2,1,0:T(8,128)(2,1)S(1)}, bf16[1,21,128,128]{3,2,1,0:T(8,128)(2,1)}, u32[]{:S(2)}) %copy-start.1) | copy-done | bytes 688152
  3.6 0.0 copy-start.2
  3.6 1.1 %copy-done.2 = bf16[1,100,2688]{2,1,0:T(8,128)(2,1)S(1)} copy-done((bf16[1,100,2688]{2,1,0:T(8,128)(2,1)S(1)}, bf16[1,100,2688]{2,1,0:T(8,128)(2,1)}, u32[]{:S(2)}) %copy-start.2) | copy-done | bytes 537624
  4.6 0.0 copy-start.3
  4.6 0.9 %copy-done.3 = bf16[4,2,128,128]{3,2,1,0:T(8,128)(2,1)S(1)} copy-done((bf16[4,2,128,128]{3,2,1,0:T(8,128)(2,1)S(1)}, bf16[4,2,128,128]{3,2,1,0:T(8,128)(2,1)}, u32[]{:S(2)}) %copy-start.3) | copy-done | bytes 262168
  5.6 0.0 copy-start.4
  5.6 0.8 copy-done.4
  6.4 0.0 copy-start.5
  6.4 0.8 copy-done.5
  7.1 67.2 %shard_map.113 = (bf16[2,5,160,100]{3,2,1,0:T(8,128)(2,1)S(1)}, f32[64,128]{1,0:T(8,128)S(1)}) custom-call(bf16[1,100,2688]{2,1,0:T(8,128)(2,1)S(1)} %copy-done.2, bf16[5,128,640]{2,1,0:T(8,128)(2,1)S(1)} %copy-done, bf16[1,21,128,128]{3,2,1,0:T(8,128)(2,1)S(1)} %copy-done.1, bf16[4,2,128,128]{3,2,1,0:T(8,128)(2,1)S(1)} %copy-done.3, f32[64,128]{1,0:T(8,128)S(1)} %bitcast.7, ...), custom_call_target="tpu_custom_call" | custom-call | flops 1000000000 | bytes 3000000 | tf_op jit(solution)/shard_map/pallas_call | solution.py:669
  74.3 0.8 copy.14
  75.1 0.6 copy.15
Async XLA Ops:
  0.6 0.7 copy-start.7
  0.6 0.7 copy-start.6
  0.7 0.7 copy-start.8
  0.7 0.7 copy-start.9
  1.3 1.1 %copy-start = (bf16[5,128,640]{2,1,0:T(8,128)(2,1)S(1)}, bf16[5,128,640]{2,1,0:T(8,128)(2,1)}, u32[]{:S(2)}) copy-start(bf16[5,128,640]{2,1,0:T(8,128)(2,1)} %poly_hbm.1) | copy-start | bytes 2457604
  2.5 1.1 %copy-start.1 = (bf16[1,21,128,128]{3,2,1,0:T(8,128)(2,1)S(1)}, bf16[1,21,128,128]{3,2,1,0:T(8,128)(2,1)}, u32[]{:S(2)}) copy-start(bf16[1,21,128,128]{3,2,1,0:T(8,128)(2,1)} %s2a_hbm.1) | copy-start | bytes 2064388
  3.6 1.1 %copy-start.2 = (bf16[1,100,2688]{2,1,0:T(8,128)(2,1)S(1)}, bf16[1,100,2688]{2,1,0:T(8,128)(2,1)}, u32[]{:S(2)}) copy-start(bf16[1,100,2688]{2,1,0:T(8,128)(2,1)} %phys_hbm.1) | copy-start | bytes 1612804
  4.6 0.9 %copy-start.3 = (bf16[4,2,128,128]{3,2,1,0:T(8,128)(2,1)S(1)}, bf16[4,2,128,128]{3,2,1,0:T(8,128)(2,1)}, u32[]{:S(2)}) copy-start(bf16[4,2,128,128]{3,2,1,0:T(8,128)(2,1)} %a2s_hbm.1) | copy-start | bytes 786436
  5.6 0.8 %copy-start.4 = (f32[2,8,4,128]{3,2,1,0:T(4,128)S(1)}, f32[2,8,4,128]{3,2,1,0:T(4,128)}, u32[]{:S(2)}) copy-start(f32[2,8,4,128]{3,2,1,0:T(4,128)} %param.13) | copy-start | bytes 98308
  6.4 0.8 %copy-start.5 = (f32[2,8,4,128]{3,2,1,0:T(4,128)S(1)}, f32[2,8,4,128]{3,2,1,0:T(4,128)}, u32[]{:S(2)}) copy-start(f32[2,8,4,128]{3,2,1,0:T(4,128)} %param.14) | copy-start | bytes 98308

commit v2 on v1

--- a/solution.py
+++ b/solution.py
@@ -94,6 +94,10 @@
     right_hand,
     got32,
     product2,
+    product0,
+    plane32,
+    select_z,
+    select_y,
     poly_t,
     flux_send,
     flux_got,
@@ -118,6 +122,10 @@
     core_got,
     outbox,
     inbox,
+    plane_send,
+    plane_got,
+    mixed_send,
+    mixed_got,
     local_sem,
     flux_ss,
     flux_rs,
@@ -135,7 +143,12 @@
     all_rs,
     ring_ss,
     ring_rs,
+    plane_ss,
+    plane_rs,
+    mixed_ss,
+    mixed_rs,
     ready,
+    ready2,
 ):
     x = lax.axis_index("grp")
     row = lax.axis_index("row")
@@ -267,25 +280,50 @@
             segments[i * PITCH : (i + 1) * PITCH, width:SEG] = jnp.zeros((PITCH, SEG - width), BF16)
         segments[i * PITCH : i * PITCH + PLANES, 0:width] = values
 
-    ins[1].wait()
-    for k in range(WAVES):
-        turned = pv[k].astype(F32).T.astype(BF16)
-        for g in range(NX):
-            poly_t[g, k * DEGREES : (k + 1) * DEGREES, :] = turned[g * DEGREES : (g + 1) * DEGREES]
-    poly_got[0] = poly_t[x]
-    poly_copies = [
-        remote(
-            poly_t.at[lax.rem(x + i, NX)],
-            poly_got.at[i],
-            poly_ss.at[i - 1],
-            poly_rs.at[i - 1],
-            x_ring[i - 1],
-        )
-        for i in range(1, NX)
-    ]
-    for copy in poly_copies:
-        copy.start()
-
+    inverse_row = 1.0 / jnp.full((1, SPAN), n, jnp.int32).astype(F32)
+    d_row = lax.broadcasted_iota(jnp.int32, (1, SPAN), 1)
+    owner_row = (d_row & 3) * 32 + ((d_row >> 2) & 15) * 2 + (d_row >> 6)
+
+    def scale_of(k):
+        return jnp.where(2 * (owner_row * WAVES + k) < n, inverse_row, 0.0)
+
+    def transform(k, _):
+        product[...] = jnp.dot(segments[...], waves[k], preferred_element_type=F32)
+        real = jnp.zeros((PITCH, SPAN), F32)
+        imag = jnp.zeros((PITCH, SPAN), F32)
+        for i in range(SEGS):
+            wc = table_c[k, 32 + i : 33 + i, :]
+            ws = table_s[k, 32 + i : 33 + i, :]
+            yc = product[i * PITCH : (i + 1) * PITCH, 0:SPAN]
+            ys = product[i * PITCH : (i + 1) * PITCH, SPAN : 2 * SPAN]
+            real = real + (yc * wc - ys * ws)
+            imag = imag + (yc * ws + ys * wc)
+        scale = scale_of(k)
+        fourier[k, 0] = real * scale
+        fourier[k, 1] = imag * scale
+        return 0
+
+    lax.fori_loop(0, WAVES, transform, 0)
+
+    for c in range(2):
+        for q in range(PARTS):
+            r = c * PARTS + q
+            parts[r, 120:128, :] = jnp.zeros((8, SPAN), F32)
+            for k in range(WAVES):
+                parts[r, k * PART : (k + 1) * PART, :] = fourier[
+                    k, c, q * PART : (q + 1) * PART, :
+                ]
+            packed32[pl.ds(r, LATS, stride=PACKED), :] = parts[r].T
+
+    half_rows = CHIPS * PACKED
+    core_send[...] = packed32[pl.ds(pl.multiple_of((1 - core) * half_rows, 8), half_rows), :].astype(
+        BF16
+    )
+    core_copy = remote(core_send, core_got, core_ss, core_rs, sibling)
+    core_copy.start()
+    mine = packed32[pl.ds(pl.multiple_of(core * half_rows, 8), half_rows), :].reshape(
+        CHIPS, PACKED, SPAN
+    )
     ins[2].wait()
     for copy in flux_copies:
         copy.wait_recv()
@@ -386,30 +424,67 @@
     for copy in halo2_copies:
         copy.start()
 
-    inverse_row = 1.0 / jnp.full((1, SPAN), n, jnp.int32).astype(F32)
-    d_row = lax.broadcasted_iota(jnp.int32, (1, SPAN), 1)
-    owner_row = (d_row & 3) * 32 + ((d_row >> 2) & 15) * 2 + (d_row >> 6)
-
-    def scale_of(k):
-        return jnp.where(2 * (owner_row * WAVES + k) < n, inverse_row, 0.0)
-
-    def transform(k, _):
-        product[...] = jnp.dot(segments[...], waves[k], preferred_element_type=F32)
-        real = jnp.zeros((PITCH, SPAN), F32)
-        imag = jnp.zeros((PITCH, SPAN), F32)
-        for i in range(SEGS):
-            wc = table_c[k, 32 + i : 33 + i, :]
-            ws = table_s[k, 32 + i : 33 + i, :]
-            yc = product[i * PITCH : (i + 1) * PITCH, 0:SPAN]
-            ys = product[i * PITCH : (i + 1) * PITCH, SPAN : 2 * SPAN]
-            real = real + (yc * wc - ys * ws)
-            imag = imag + (yc * ws + ys * wc)
-        scale = scale_of(k)
-        fourier[k, 0] = real * scale
-        fourier[k, 1] = imag * scale
+    core_copy.wait_recv()
+    theirs = core_got[...].astype(F32).reshape(CHIPS, PACKED, SPAN)
+    is_first = core == 0
+    out32[:, 0:PACKED, :] = jnp.where(is_first, mine, theirs)
+    out32[:, PACKED : 2 * PACKED, :] = jnp.where(is_first, theirs, mine)
+    outbox[...] = out32[...].astype(BF16)
+    pl.semaphore_wait(ready, NY - 1)
+    for device in x_ring:
+        pl.semaphore_signal(ready2, inc=1, device_id=device, device_id_type=MESH)
+
+    def post(i, _):
+        zz = lax.rem(z + i, NZ)
+        for j in range(NY):
+            yy = lax.rem(y + j, NY)
+            remote(
+                outbox.at[zz * NY + yy],
+                inbox.at[0, y, z],
+                all_ss,
+                all_rs.at[j],
+                at(x, yy, zz, core),
+            ).start()
         return 0
 
-    lax.fori_loop(0, 3, transform, 0)
+    lax.fori_loop(1, NZ, post, 0)
+    for j in range(1, NY):
+        yy = lax.rem(y + j, NY)
+        remote(
+            outbox.at[z * NY + yy], inbox.at[0, y, z], all_ss, all_rs.at[j], at(x, yy, z, core)
+        ).start()
+    inbox[0, pl.ds(y, 1), pl.ds(z, 1)] = outbox[pl.ds(z * NY + y, 1)][None]
+
+    ins[1].wait()
+    for k in range(WAVES):
+        turned = pv[k].astype(F32).T.astype(BF16)
+        for g in range(NX):
+            poly_t[g, k * DEGREES : (k + 1) * DEGREES, :] = turned[g * DEGREES : (g + 1) * DEGREES]
+    poly_got[0] = poly_t[x]
+    poly_copies = [
+        remote(
+            poly_t.at[lax.rem(x + i, NX)],
+            poly_got.at[i],
+            poly_ss.at[i - 1],
+            poly_rs.at[i - 1],
+            x_ring[i - 1],
+        )
+        for i in range(1, NX)
+    ]
+    for copy in poly_copies:
+        copy.start()
+
+    rows_a = lax.broadcasted_iota(jnp.int32, (NZ * SPAN, SPAN), 0)
+    lanes_a = lax.broadcasted_iota(jnp.int32, (NZ * SPAN, SPAN), 1)
+    wanted = ((lanes_a >> 2) & 1) * CHIPS + z * NY + (lanes_a & 3)
+    chosen = ((rows_a >> 7) == (lanes_a >> 3)) & ((rows_a & 127) == wanted)
+    select_z[...] = jnp.where(chosen, 1.0, 0.0).astype(BF16)
+    rows_b = lax.broadcasted_iota(jnp.int32, (8 * SPAN, SPAN), 0)
+    lanes_b = lax.broadcasted_iota(jnp.int32, (8 * SPAN, SPAN), 1)
+    lane_in = rows_b & 127
+    wanted = (rows_b >> 8) * 32 + (lane_in >> 3) * 2 + ((rows_b >> 7) & 1)
+    chosen = ((lane_in & 7) == core * 4 + y) & (lanes_b == wanted)
+    select_y[...] = jnp.where(chosen, 1.0, 0.0).astype(BF16)
 
     for copy in halo2_copies:
         copy.wait_recv()
@@ -429,8 +504,6 @@
     ]
     for copy in sst_copies:
         copy.start()
-
-    lax.fori_loop(3, WAVES, transform, 0)
 
     ins[3].wait()
     for copy in sst_copies:
@@ -448,6 +521,7 @@
         half = (b % 2) * SPAN
         row0[b // 2 : b // 2 + 1, half : half + SPAN] = plane
     surface = row0[...].astype(BF16)
+    plane32[...] = jnp.zeros_like(plane32)
     for k in range(WAVES):
         part = jnp.dot(surface, waves[k], preferred_element_type=F32)
         wc = table_c[k, 32:48, :]
@@ -455,73 +529,87 @@
         yc = part[:, 0:SPAN]
         ys = part[:, SPAN : 2 * SPAN]
         scale = scale_of(k)
-        fourier[k, 0, 0:1, :] = jnp.sum(yc * wc - ys * ws, axis=0, keepdims=True) * scale
-        fourier[k, 1, 0:1, :] = jnp.sum(yc * ws + ys * wc, axis=0, keepdims=True) * scale
-
-    for c in range(2):
-        for q in range(PARTS):
-            r = c * PARTS + q
-            parts[r, 120:128, :] = jnp.zeros((8, SPAN), F32)
-            for k in range(WAVES):
-                parts[r, k * PART : (k + 1) * PART, :] = fourier[
-                    k, c, q * PART : (q + 1) * PART, :
-                ]
-            packed32[pl.ds(r, LATS, stride=PACKED), :] = parts[r].T
-
-    half_rows = CHIPS * PACKED
-    core_send[...] = packed32[pl.ds(pl.multiple_of((1 - core) * half_rows, 8), half_rows), :].astype(
-        BF16
-    )
-    core_copy = remote(core_send, core_got, core_ss, core_rs, sibling)
-    core_copy.start()
-    mine = packed32[pl.ds(pl.multiple_of(core * half_rows, 8), half_rows), :].reshape(
-        CHIPS, PACKED, SPAN
-    )
-    core_copy.wait_recv()
-    theirs = core_got[...].astype(F32).reshape(CHIPS, PACKED, SPAN)
-    is_first = core == 0
-    out32[:, 0:PACKED, :] = jnp.where(is_first, mine, theirs)
-    out32[:, PACKED : 2 * PACKED, :] = jnp.where(is_first, theirs, mine)
-    outbox[...] = out32[...].astype(BF16)
-    pl.semaphore_wait(ready, NY - 1)
-    me = y * NZ + z
-
-    def post(i, _):
-        zz = lax.rem(z + i, NZ)
-        for j in range(NY):
-            yy = lax.rem(y + j, NY)
-            remote(
-                outbox.at[zz * NY + yy], inbox.at[0, me], all_ss, all_rs, at(x, yy, zz, core)
-            ).start()
-        return 0
-
-    lax.fori_loop(1, NZ, post, 0)
-    for j in range(1, NY):
-        yy = lax.rem(y + j, NY)
-        remote(outbox.at[z * NY + yy], inbox.at[0, me], all_ss, all_rs, at(x, yy, z, core)).start()
-    inbox[0, pl.ds(me, 1)] = outbox[pl.ds(z * NY + y, 1)]
-
-    for copy in flux_copies + halo_copies + halo2_copies + sst_copies + poly_copies:
-        copy.wait_send()
-    core_copy.wait_send()
-    for copy in poly_copies:
-        copy.wait_recv()
-    degrees = jnp.concatenate([poly_got[i] for i in range(NX)], axis=1)
-
-    every = remote(
-        outbox.at[pl.ds(0, CHIPS - 1)],
-        inbox.at[0, pl.ds(0, CHIPS - 1)],
-        all_ss,
-        all_rs,
-        sibling,
-    )
-    every.wait_recv()
+        plane32[2 * k : 2 * k + 1, :] = jnp.sum(yc * wc - ys * ws, axis=0, keepdims=True) * scale
+        plane32[2 * k + 1 : 2 * k + 2, :] = (
+            jnp.sum(yc * ws + ys * wc, axis=0, keepdims=True) * scale
+        )
+
+    plane_send[...] = plane32[...].astype(BF16)
+    plane_got[pl.ds(z, 1)] = plane_send[...][None]
+    for device in z_ring:
+        remote(plane_send, plane_got.at[z], plane_ss, plane_rs, device).start()
+
     next_x = x_ring[0]
     last_x = x_ring[-1]
-    ring_right = remote(inbox.at[0], inbox.at[1], ring_ss.at[0], ring_rs.at[0], next_x)
-    ring_left = remote(inbox.at[0], inbox.at[3], ring_ss.at[1], ring_rs.at[1], last_x)
-    ring_right.start()
-    ring_left.start()
+    ring_right = []
+    ring_left = []
+    ring_on = []
+
+    def circulate(j):
+        count = NZ - 1 if j == 0 else NZ
+        arrived = remote(
+            outbox.at[pl.ds(0, count)],
+            inbox.at[0, 0, pl.ds(0, count)],
+            all_ss,
+            all_rs.at[j],
+            sibling,
+        )
+        arrived.wait_recv()
+        yy = lax.rem(y + NY - j, NY)
+        to_right = remote(
+            inbox.at[0, yy], inbox.at[1, yy], ring_ss.at[0, j], ring_rs.at[0, j], next_x
+        )
+        to_left = remote(
+            inbox.at[0, yy], inbox.at[3, yy], ring_ss.at[1, j], ring_rs.at[1, j], last_x
+        )
+        to_right.start()
+        to_left.start()
+        ring_right.append(to_right)
+        ring_left.append(to_left)
+
+    def pass_on(j):
+        yy = lax.rem(y + NY - j, NY)
+        ring_right[j].wait_recv()
+        ring_left[j].wait_recv()
+        slot, device = (1, next_x) if j % 2 == 0 else (3, last_x)
+        copy = remote(
+            inbox.at[slot, yy], inbox.at[2, yy], ring_ss.at[2, j], ring_rs.at[2, j], device
+        )
+        copy.start()
+        ring_on.append(copy)
+
+    circulate(0)
+    circulate(1)
+    circulate(2)
+    pass_on(0)
+    circulate(3)
+    pass_on(1)
+
+    def many(copies, device):
+        return remote(
+            plane_got.at[pl.ds(0, copies)],
+            plane_got.at[pl.ds(0, copies)],
+            plane_ss,
+            plane_rs,
+            device,
+        )
+
+    many(NZ - 1, sibling).wait_recv()
+    stretch = jnp.concatenate([plane_got[i] for i in range(NZ)], axis=1)
+    mixed = jnp.dot(stretch, select_z[...], preferred_element_type=F32).astype(BF16)
+    mixed_send[...] = mixed
+    pl.semaphore_wait(ready2, NX - 1)
+    mixed_got[pl.ds(y * 2 + core, 1)] = mixed[None]
+    for i in range(1, NX * NY * NCORE):
+        dx, dy, dc = i // 8, (i // 2) % 4, i % 2
+        cc = 1 - core if dc else core
+        remote(
+            mixed_send,
+            mixed_got.at[dx * 8 + y * 2 + core],
+            mixed_ss,
+            mixed_rs,
+            at(lax.rem(x + dx, NX), lax.rem(y + dy, NY), z, cc),
+        ).start()
 
     def unpack(slot):
         got32[...] = inbox[slot].astype(F32).reshape(CHIPS * 2 * PACKED, SPAN)
@@ -531,51 +619,75 @@
             ].astype(BF16)
 
     unpack(0)
-    middle = CHIPS // 2
-    ring_right.wait_recv()
-    on_right = remote(
-        inbox.at[1, pl.ds(0, middle)],
-        inbox.at[2, pl.ds(0, middle)],
-        ring_ss.at[2],
-        ring_rs.at[2],
-        next_x,
-    )
-    on_right.start()
-    ring_left.wait_recv()
-    on_left = remote(
-        inbox.at[3, pl.ds(middle, middle)],
-        inbox.at[2, pl.ds(middle, middle)],
-        ring_ss.at[3],
-        ring_rs.at[3],
-        last_x,
-    )
-    on_left.start()
+    pass_on(2)
+    pass_on(3)
     unpack(1)
     unpack(3)
-    on_right.wait_recv()
-    on_left.wait_recv()
+    for copy in poly_copies:
+        copy.wait_recv()
+    degrees = jnp.concatenate([poly_got[i] for i in range(NX)], axis=1)
+    for copy in ring_on:
+        copy.wait_recv()
     unpack(2)
 
-    lanes = lax.broadcasted_iota(jnp.int32, (DEGREES, SPAN), 1)
     for c in range(2):
         for pair in range(2):
             start = (c * PARTS + pair * 2) * SPAN
-            product2[:, pair * 2 * SPAN : (pair + 1) * 2 * SPAN] = jnp.dot(
+            product2[:, start : start + 2 * SPAN] = jnp.dot(
                 degrees, right_hand[:, start : start + 2 * SPAN], preferred_element_type=F32
             )
+    remote(
+        mixed_got.at[pl.ds(0, 31)], mixed_got.at[pl.ds(0, 31)], mixed_ss, mixed_rs, sibling
+    ).wait_recv()
+    stacked = jnp.concatenate(
+        [
+            jnp.concatenate([mixed_got[slot * 8 + i] for i in range(8)], axis=1)
+            for slot in range(NX)
+        ],
+        axis=0,
+    )
+    sorted_rows = jnp.dot(stacked, select_y[...], preferred_element_type=F32).astype(BF16)
+    surface_rows = jnp.concatenate(
+        [sorted_rows[slot * 16 : (slot + 1) * 16, :] for slot in range(NX)], axis=1
+    )
+    surface_rows = jnp.concatenate(
+        [surface_rows, jnp.zeros((SPAN - 16, NX * LATS), BF16)], axis=0
+    )
+    product0[...] = dot_t(degrees, surface_rows)
+    lanes = lax.broadcasted_iota(jnp.int32, (DEGREES, SPAN), 1)
+    for c in range(2):
         for k in range(WAVES):
             total = jnp.zeros((DEGREES, SPAN), F32)
             for q in range(PARTS):
-                block = product2[k * DEGREES : (k + 1) * DEGREES, q * SPAN : (q + 1) * SPAN]
+                r = c * PARTS + q
+                block = product2[k * DEGREES : (k + 1) * DEGREES, r * SPAN : (r + 1) * SPAN]
                 turn = (PART * (q - k)) % SPAN
                 if turn:
                     block = pltpu.roll(block, turn, 1)
                 keep = (lanes >= q * PART) & (lanes < (q + 1) * PART)
                 total = jnp.where(keep, block, total)
+            block = product0[k * DEGREES : (k + 1) * DEGREES, :]
+            turn = (-(2 * k + c)) % SPAN
+            if turn:
+                block = pltpu.roll(block, turn, 1)
+            total = jnp.where(lanes == 0, block, total)
             spectral_ref[c, k] = total[:, 0:PLANES].astype(BF16)
 
-    every.wait_send()
-    for copy in (ring_right, ring_left, on_right, on_left):
+    for copy in flux_copies + halo_copies + halo2_copies + sst_copies + poly_copies:
+        copy.wait_send()
+    core_copy.wait_send()
+    remote(
+        outbox.at[pl.ds(0, CHIPS - 1)],
+        outbox.at[pl.ds(0, CHIPS - 1)],
+        all_ss,
+        all_rs.at[0],
+        sibling,
+    ).wait_send()
+    many(NZ - 1, sibling).wait_send()
+    remote(
+        mixed_got.at[pl.ds(0, 31)], mixed_got.at[pl.ds(0, 31)], mixed_ss, mixed_rs, sibling
+    ).wait_send()
+    for copy in ring_right + ring_left + ring_on:
         copy.wait_send()
 
 
@@ -622,7 +734,11 @@
         pltpu.VMEM((CHIPS, 2 * PACKED, SPAN), F32),
         pltpu.VMEM((NX * LATS, PACKED * SPAN), BF16),
         pltpu.VMEM((LATS * PACKED, SPAN), F32),
-        pltpu.VMEM((WAVES * DEGREES, PARTS * SPAN), F32),
+        pltpu.VMEM((WAVES * DEGREES, PACKED * SPAN), F32),
+        pltpu.VMEM((WAVES * DEGREES, SPAN), F32),
+        pltpu.VMEM((16, SPAN), F32),
+        pltpu.VMEM((NZ * SPAN, SPAN), BF16),
+        pltpu.VMEM((8 * SPAN, SPAN), BF16),
         pltpu.VMEM((NX, WAVES * DEGREES, LATS), BF16),
         pltpu.VMEM((48, SPAN), BF16),
         pltpu.VMEM((NCOL, 48, SPAN), BF16),
@@ -646,7 +762,11 @@
         pltpu.VMEM((CHIPS * PACKED, SPAN), BF16),
         pltpu.VMEM((CHIPS * PACKED, SPAN), BF16),
         pltpu.VMEM((CHIPS, 2 * PACKED, SPAN), BF16),
-        pltpu.VMEM((NX, CHIPS, 2 * PACKED, SPAN), BF16),
+        pltpu.VMEM((NX, NY, NZ, 2 * PACKED, SPAN), BF16),
+        pltpu.VMEM((16, SPAN), BF16),
+        pltpu.VMEM((NZ, 16, SPAN), BF16),
+        pltpu.VMEM((16, SPAN), BF16),
+        pltpu.VMEM((NX * NY * NCORE, 16, SPAN), BF16),
         dma((4,)),
         dma((NCOL - 1,)),
         dma((NCOL - 1,)),
@@ -661,9 +781,14 @@
         dma,
         dma,
         dma,
+        dma((NY,)),
+        dma((3, NY)),
+        dma((3, NY)),
         dma,
-        dma((4,)),
-        dma((4,)),
+        dma,
+        dma,
+        dma,
+        pltpu.SemaphoreType.REGULAR,
         pltpu.SemaphoreType.REGULAR,
     ]
     spectral, tracers = pl.pallas_call(
@@ -676,7 +801,7 @@
         out_specs=(vmem, vmem),
         scratch_shapes=scratch,
         compiler_params=pltpu.CompilerParams(
-            collective_id=0, has_side_effects=True, vmem_limit_bytes=48 * 2**20
+            collective_id=0, has_side_effects=True, vmem_limit_bytes=64 * 2**20
         ),
         cost_estimate=pl.CostEstimate(
             flops=1_000_000_000, bytes_accessed=3_000_000, transcendentals=0

time: 76.2 us -> 59.6 us (0.78)
  the two profiles are of different devices: /device:TPU:2 before, /device:TPU:1 now
where the time goes in v2:
time: 59.6 us; the launch traced here: 59.3 us
  Pallas kernels  56.3 us (94%)
  local copies, waits for them, and re-layouts  2.4 us (4%)
  between operations  0.65 us (1%)
    pallas_call x1, Pallas kernels, local(): pl.pallas_call(kernel, out_shape=(jax.ShapeDtypeStruct((2, WAVES, DEGREES...  56.3 us
    unnamed x4, local copies, waits for them, and re-layouts  2.4 us

profile of v2, /device:TPU:1, one launch (start us, length us, event | category | flops | bytes accessed | tf_op | source)
XLA Modules:
  0.0 59.3 jit_solution(5050026599118153012)
XLA Ops:
  0.6 56.3 %shard_map.113 = (bf16[2,5,160,100]{3,2,1,0:T(8,128)(2,1)}, f32[64,128]{1,0:T(8,128)}) custom-call(bf16[1,100,2688]{2,1,0:T(8,128)(2,1)} %phys_hbm.1, bf16[5,128,640]{2,1,0:T(8,128)(2,1)} %poly_hbm.1, bf16[1,21,128,128]{3,2,1,0:T(8,128)(2,1)} %s2a_hbm.1, bf16[4,2,128,128]{3,2,1,0:T(8,128)(2,1)} %a2s_hbm.1, f32[64,128]{1,0:T(8,128)} %bitcast.7, ...), custom_call_target="tpu_custom_call" | custom-call | flops 1000000000 | bytes 3000000 | tf_op jit(solution)/shard_map/pallas_call | solution.py:794
  56.9 0.0 copy-start
  56.9 1.8 %copy.14 = bf16[100,2,5,160]{0,3,2,1:T(8,128)(2,1)} copy(bf16[100,2,5,160]{0,3,2,1:T(8,128)(2,1)} %bitcast.5) | data formatting | bytes 640000
  58.7 0.0 copy-done
  58.7 0.6 %copy.15 = f32[2,8,4,128]{3,2,1,0:T(4,128)} copy(f32[2,8,4,128]{3,2,1,0:T(4,128)S(1)} %bitcast.6) | data formatting | bytes 65536
Async XLA Ops:
  56.9 1.8 %copy-start = (f32[64,128]{1,0:T(8,128)S(1)}, f32[64,128]{1,0:T(8,128)}, u32[]{:S(2)}) copy-start(f32[64,128]{1,0:T(8,128)} %get-tuple-element.5) | copy-start | bytes 98308

commit v3 on v2

--- a/solution.py
+++ b/solution.py
@@ -59,15 +59,24 @@
     poly_hbm,
     s2a_hbm,
     a2s_hbm,
+    tracer_hbm,
+    courant_hbm,
+    water_hbm,
+    points_hbm,
+    air_hbm,
+    sea_hbm,
+    spectral_hbm,
+    tracer_out_hbm,
+    spectral_ref,
+    tracer_out_ref,
     tracer_ref,
     courant_ref,
     water_ref,
     points_ref,
     air_ref,
     sea_ref,
-    spectral_ref,
-    tracer_out_ref,
     xv,
+    xtop,
     pv,
     s2av,
     a2sv,
@@ -96,8 +105,8 @@
     product2,
     product0,
     plane32,
-    select_z,
     select_y,
+    bulk,
     poly_t,
     flux_send,
     flux_got,
@@ -179,25 +188,37 @@
     x_ring = [at(lax.rem(x + i, NX), y, z, core) for i in range(1, NX)]
     sibling = at(x, y, z, 1 - core)
 
+    moves = [
+        (phys_hbm, xv),
+        (poly_hbm, pv),
+        (a2s_hbm, a2sv),
+        (s2a_hbm, s2av),
+        (points_hbm, points_ref),
+        (phys_hbm.at[0, pl.ds(0, 32)], xtop),
+        (tracer_hbm, tracer_ref),
+        (courant_hbm, courant_ref),
+        (water_hbm, water_ref),
+        (air_hbm, air_ref),
+        (sea_hbm, sea_ref),
+    ]
     ins = [
-        pltpu.make_async_copy(phys_hbm, xv, local_sem.at[0]),
-        pltpu.make_async_copy(poly_hbm, pv, local_sem.at[1]),
-        pltpu.make_async_copy(a2s_hbm, a2sv, local_sem.at[2]),
-        pltpu.make_async_copy(s2a_hbm, s2av, local_sem.at[3]),
+        pltpu.make_async_copy(source, target, local_sem.at[i])
+        for i, (source, target) in enumerate(moves)
     ]
-    for copy in ins:
-        copy.start()
+    for i in (4, 5, 6, 7, 8, 0, 9, 2, 10, 3, 1):
+        ins[i].start()
     barrier = pltpu.get_barrier_semaphore()
     greeted = band + [below, above, sibling] + x_ring + y_ring + z_ring
     for device in greeted:
         pl.semaphore_signal(barrier, inc=1, device_id=device, device_id_type=MESH)
 
     own = strip * NCOL + col
+    ins[4].wait()
     n = points_ref[own]
     lane = lax.broadcasted_iota(jnp.int32, (1, SPAN), 1)
 
-    ins[0].wait()
-    x32[...] = xv[0, 0:32, :].astype(F32)
+    ins[5].wait()
+    x32[...] = xtop[...].astype(F32)
     flux32[...] = jnp.zeros_like(flux32)
     for b in range(SPANS):
         live = lane + b * SPAN < n
@@ -207,6 +228,8 @@
     flux_send[...] = flux32[...].astype(BF16)
     flux_got[pl.ds(col, 1)] = flux_send[...][None]
 
+    for i in (6, 7, 8):
+        ins[i].wait()
     wet = water_ref[...].astype(F32)
     for i in range(16):
         cells32[96 + 4 * i : 100 + 4 * i, :] = wet
@@ -270,6 +293,7 @@
 
     lax.fori_loop(0, 16, fill_waves, 0)
 
+    ins[0].wait()
     for i in range(SEGS):
         width = min(SEG, POINTS - i * SEG)
         pos = i * SEG + lax.broadcasted_iota(jnp.int32, (1, width), 1)
@@ -325,6 +349,7 @@
         CHIPS, PACKED, SPAN
     )
     ins[2].wait()
+    ins[9].wait()
     for copy in flux_copies:
         copy.wait_recv()
     flux_got32[...] = flux_got[...].astype(F32)
@@ -434,10 +459,11 @@
     for device in x_ring:
         pl.semaphore_signal(ready2, inc=1, device_id=device, device_id_type=MESH)
 
-    def post(i, _):
-        zz = lax.rem(z + i, NZ)
-        for j in range(NY):
-            yy = lax.rem(y + j, NY)
+    for j in range(NY):
+        yy = lax.rem(y + j, NY)
+
+        def post(i, _, j=j, yy=yy):
+            zz = lax.rem(z + i, NZ)
             remote(
                 outbox.at[zz * NY + yy],
                 inbox.at[0, y, z],
@@ -445,14 +471,11 @@
                 all_rs.at[j],
                 at(x, yy, zz, core),
             ).start()
-        return 0
-
-    lax.fori_loop(1, NZ, post, 0)
-    for j in range(1, NY):
-        yy = lax.rem(y + j, NY)
-        remote(
-            outbox.at[z * NY + yy], inbox.at[0, y, z], all_ss, all_rs.at[j], at(x, yy, z, core)
-        ).start()
+            return 0
+
+        lax.fori_loop(1, NZ, post, 0)
+        if j:
+            post(0, 0)
     inbox[0, pl.ds(y, 1), pl.ds(z, 1)] = outbox[pl.ds(z * NY + y, 1)][None]
 
     ins[1].wait()
@@ -474,11 +497,6 @@
     for copy in poly_copies:
         copy.start()
 
-    rows_a = lax.broadcasted_iota(jnp.int32, (NZ * SPAN, SPAN), 0)
-    lanes_a = lax.broadcasted_iota(jnp.int32, (NZ * SPAN, SPAN), 1)
-    wanted = ((lanes_a >> 2) & 1) * CHIPS + z * NY + (lanes_a & 3)
-    chosen = ((rows_a >> 7) == (lanes_a >> 3)) & ((rows_a & 127) == wanted)
-    select_z[...] = jnp.where(chosen, 1.0, 0.0).astype(BF16)
     rows_b = lax.broadcasted_iota(jnp.int32, (8 * SPAN, SPAN), 0)
     lanes_b = lax.broadcasted_iota(jnp.int32, (8 * SPAN, SPAN), 1)
     lane_in = rows_b & 127
@@ -496,6 +514,8 @@
         right2[...].astype(F32) * has_right,
     )
     tracer_out_ref[...] = state
+    tracer_leave = pltpu.make_async_copy(tracer_out_ref, tracer_out_hbm, local_sem.at[11])
+    tracer_leave.start()
     sst_send[...] = state[0:16, :].astype(BF16)
     sst_got[pl.ds(col, 1)] = sst_send[...][None]
     sst_copies = [
@@ -505,7 +525,50 @@
     for copy in sst_copies:
         copy.start()
 
+    next_x = x_ring[0]
+    last_x = x_ring[-1]
+    ring_right = []
+    ring_left = []
+    ring_on = []
+
+    def circulate(j):
+        count = NZ - 1 if j == 0 else NZ
+        arrived = remote(
+            outbox.at[pl.ds(0, count)],
+            inbox.at[0, 0, pl.ds(0, count)],
+            all_ss,
+            all_rs.at[j],
+            sibling,
+        )
+        arrived.wait_recv()
+        yy = lax.rem(y + NY - j, NY)
+        to_right = remote(
+            inbox.at[0, yy], inbox.at[1, yy], ring_ss.at[0, j], ring_rs.at[0, j], next_x
+        )
+        to_left = remote(
+            inbox.at[0, yy], inbox.at[3, yy], ring_ss.at[1, j], ring_rs.at[1, j], last_x
+        )
+        to_right.start()
+        to_left.start()
+        ring_right.append(to_right)
+        ring_left.append(to_left)
+
+    def pass_on(j):
+        yy = lax.rem(y + NY - j, NY)
+        ring_right[j].wait_recv()
+        ring_left[j].wait_recv()
+        slot, device = (1, next_x) if j % 2 == 0 else (3, last_x)
+        copy = remote(
+            inbox.at[slot, yy], inbox.at[2, yy], ring_ss.at[2, j], ring_rs.at[2, j], device
+        )
+        copy.start()
+        ring_on.append(copy)
+
+    circulate(0)
+    circulate(1)
+
     ins[3].wait()
+    ins[10].wait()
     for copy in sst_copies:
         copy.wait_recv()
     sst_got32[...] = sst_got[...].astype(F32)
@@ -539,47 +602,6 @@
     for device in z_ring:
         remote(plane_send, plane_got.at[z], plane_ss, plane_rs, device).start()
 
-    next_x = x_ring[0]
-    last_x = x_ring[-1]
-    ring_right = []
-    ring_left = []
-    ring_on = []
-
-    def circulate(j):
-        count = NZ - 1 if j == 0 else NZ
-        arrived = remote(
-            outbox.at[pl.ds(0, count)],
-            inbox.at[0, 0, pl.ds(0, count)],
-            all_ss,
-            all_rs.at[j],
-            sibling,
-        )
-        arrived.wait_recv()
-        yy = lax.rem(y + NY - j, NY)
-        to_right = remote(
-            inbox.at[0, yy], inbox.at[1, yy], ring_ss.at[0, j], ring_rs.at[0, j], next_x
-        )
-        to_left = remote(
-            inbox.at[0, yy], inbox.at[3, yy], ring_ss.at[1, j], ring_rs.at[1, j], last_x
-        )
-        to_right.start()
-        to_left.start()
-        ring_right.append(to_right)
-        ring_left.append(to_left)
-
-    def pass_on(j):
-        yy = lax.rem(y + NY - j, NY)
-        ring_right[j].wait_recv()
-        ring_left[j].wait_recv()
-        slot, device = (1, next_x) if j % 2 == 0 else (3, last_x)
-        copy = remote(
-            inbox.at[slot, yy], inbox.at[2, yy], ring_ss.at[2, j], ring_rs.at[2, j], device
-        )
-        copy.start()
-        ring_on.append(copy)
-
-    circulate(0)
-    circulate(1)
     circulate(2)
     pass_on(0)
     circulate(3)
@@ -595,8 +617,16 @@
         )
 
     many(NZ - 1, sibling).wait_recv()
-    stretch = jnp.concatenate([plane_got[i] for i in range(NZ)], axis=1)
-    mixed = jnp.dot(stretch, select_z[...], preferred_element_type=F32).astype(BF16)
+    stretch = plane_got[...].astype(F32).reshape(NZ * 16, SPAN)
+    stretch = pltpu.roll(stretch, lax.rem(SPAN - NY * z, SPAN), 1)
+    place = lax.broadcasted_iota(jnp.int32, (16, SPAN), 1) >> 2
+    mixed = jnp.zeros((16, SPAN), F32)
+    for i in range(NZ):
+        tile = stretch[i * 16 : (i + 1) * 16, :]
+        low = pltpu.roll(tile, 8 * i, 1) if i else tile
+        high = pltpu.roll(tile, (8 * i + 4 + CHIPS) % SPAN, 1)
+        mixed = jnp.where(place == 2 * i, low, jnp.where(place == 2 * i + 1, high, mixed))
+    mixed = mixed.astype(BF16)
     mixed_send[...] = mixed
     pl.semaphore_wait(ready2, NX - 1)
     mixed_got[pl.ds(y * 2 + core, 1)] = mixed[None]
@@ -636,24 +666,6 @@
             product2[:, start : start + 2 * SPAN] = jnp.dot(
                 degrees, right_hand[:, start : start + 2 * SPAN], preferred_element_type=F32
             )
-    remote(
-        mixed_got.at[pl.ds(0, 31)], mixed_got.at[pl.ds(0, 31)], mixed_ss, mixed_rs, sibling
-    ).wait_recv()
-    stacked = jnp.concatenate(
-        [
-            jnp.concatenate([mixed_got[slot * 8 + i] for i in range(8)], axis=1)
-            for slot in range(NX)
-        ],
-        axis=0,
-    )
-    sorted_rows = jnp.dot(stacked, select_y[...], preferred_element_type=F32).astype(BF16)
-    surface_rows = jnp.concatenate(
-        [sorted_rows[slot * 16 : (slot + 1) * 16, :] for slot in range(NX)], axis=1
-    )
-    surface_rows = jnp.concatenate(
-        [surface_rows, jnp.zeros((SPAN - 16, NX * LATS), BF16)], axis=0
-    )
-    product0[...] = dot_t(degrees, surface_rows)
     lanes = lax.broadcasted_iota(jnp.int32, (DEGREES, SPAN), 1)
     for c in range(2):
         for k in range(WAVES):
@@ -666,12 +678,40 @@
                     block = pltpu.roll(block, turn, 1)
                 keep = (lanes >= q * PART) & (lanes < (q + 1) * PART)
                 total = jnp.where(keep, block, total)
+            bulk[c, k] = total
+
+    remote(
+        mixed_got.at[pl.ds(0, 31)], mixed_got.at[pl.ds(0, 31)], mixed_ss, mixed_rs, sibling
+    ).wait_recv()
+    stacked = jnp.concatenate(
+        [
+            jnp.concatenate([mixed_got[slot * 8 + i] for i in range(8)], axis=1)
+            for slot in range(NX)
+        ],
+        axis=0,
+    )
+    sorted_rows = jnp.dot(stacked, select_y[...], preferred_element_type=F32).astype(BF16)
+    surface_rows = jnp.concatenate(
+        [sorted_rows[slot * 16 : (slot + 1) * 16, :] for slot in range(NX)], axis=1
+    )
+    surface_rows = jnp.concatenate(
+        [surface_rows, jnp.zeros((SPAN - 16, NX * LATS), BF16)], axis=0
+    )
+    product0[...] = dot_t(degrees, surface_rows)
+    leaves = [tracer_leave]
+    for c in range(2):
+        for k in range(WAVES):
             block = product0[k * DEGREES : (k + 1) * DEGREES, :]
             turn = (-(2 * k + c)) % SPAN
             if turn:
                 block = pltpu.roll(block, turn, 1)
-            total = jnp.where(lanes == 0, block, total)
+            total = jnp.where(lanes == 0, block, bulk[c, k])
             spectral_ref[c, k] = total[:, 0:PLANES].astype(BF16)
+        leave = pltpu.make_async_copy(
+            spectral_ref.at[c], spectral_hbm.at[c], local_sem.at[12 + c]
+        )
+        leave.start()
+        leaves.append(leave)
 
     for copy in flux_copies + halo_copies + halo2_copies + sst_copies + poly_copies:
         copy.wait_send()
@@ -689,6 +729,8 @@
     ).wait_send()
     for copy in ring_right + ring_left + ring_on:
         copy.wait_send()
+    for copy in leaves:
+        copy.wait()
 
 
 def local(
@@ -703,12 +745,19 @@
     sea_to_air_coefficients,
     sea_partner_span,
 ):
-    vmem = pl.BlockSpec(memory_space=pltpu.VMEM)
-    smem = pl.BlockSpec(memory_space=pltpu.SMEM)
-    anywhere = pl.BlockSpec(memory_space=pl.ANY)
+    hbm = pl.BlockSpec(memory_space=pltpu.HBM)
     dma = pltpu.SemaphoreType.DMA
     scratch = [
+        pltpu.VMEM((2, WAVES, DEGREES, PLANES), BF16),
+        pltpu.VMEM((TRACER_ROWS, SPAN), F32),
+        pltpu.VMEM((TRACER_ROWS, SPAN), F32),
+        pltpu.VMEM((TRACER_ROWS, SPAN), F32),
+        pltpu.VMEM((LINES, SPAN), jnp.int32),
+        pltpu.SMEM((512,), jnp.int32),
+        pltpu.SMEM((1, 2, LINES), jnp.int32),
+        pltpu.SMEM((1, SPANS), jnp.int32),
         pltpu.VMEM((1, PLANES, POINTS), BF16),
+        pltpu.VMEM((32, POINTS), BF16),
         pltpu.VMEM((WAVES, LATS, NX * DEGREES), BF16),
         pltpu.VMEM((1, SPANS, SPAN, SPAN), BF16),
         pltpu.VMEM((LINES, 2, SPAN, SPAN), BF16),
@@ -737,8 +786,8 @@
         pltpu.VMEM((WAVES * DEGREES, PACKED * SPAN), F32),
         pltpu.VMEM((WAVES * DEGREES, SPAN), F32),
         pltpu.VMEM((16, SPAN), F32),
-        pltpu.VMEM((NZ * SPAN, SPAN), BF16),
         pltpu.VMEM((8 * SPAN, SPAN), BF16),
+        pltpu.VMEM((2, WAVES, DEGREES, SPAN), F32),
         pltpu.VMEM((NX, WAVES * DEGREES, LATS), BF16),
         pltpu.VMEM((48, SPAN), BF16),
         pltpu.VMEM((NCOL, 48, SPAN), BF16),
@@ -767,7 +816,7 @@
         pltpu.VMEM((NZ, 16, SPAN), BF16),
         pltpu.VMEM((16, SPAN), BF16),
         pltpu.VMEM((NX * NY * NCORE, 16, SPAN), BF16),
-        dma((4,)),
+        dma((14,)),
         dma((NCOL - 1,)),
         dma((NCOL - 1,)),
         dma((4,)),
@@ -797,8 +846,8 @@
             jax.ShapeDtypeStruct((2, WAVES, DEGREES, PLANES), BF16),
             jax.ShapeDtypeStruct((TRACER_ROWS, SPAN), F32),
         ),
-        in_specs=[anywhere] * 4 + [vmem] * 3 + [smem] * 3,
-        out_specs=(vmem, vmem),
+        in_specs=[hbm] * 10,
+        out_specs=(hbm, hbm),
         scratch_shapes=scratch,
         compiler_params=pltpu.CompilerParams(
             collective_id=0, has_side_effects=True, vmem_limit_bytes=64 * 2**20

time: 59.6 us -> 56.8 us (0.953)
  Pallas kernels: 56.3 us -> 53.6 us
    pallas_call x1, Pallas kernels: 56.3 us -> 53.6 us  [local(): pl.pallas_call(kernel, out_shape=(jax.ShapeDtypeStruct((2, WAVES, DEGREES...]
where the time goes in v3:
time: 56.8 us; the launch traced here: 56.7 us
  Pallas kernels  53.6 us (94%)
  local copies, waits for them, and re-layouts  2.4 us (4%)
  between operations  0.65 us (1%)
    pallas_call x1, Pallas kernels, local(): pl.pallas_call(kernel, out_shape=(jax.ShapeDtypeStruct((2, WAVES, DEGREES...  53.6 us
    unnamed x4, local copies, waits for them, and re-layouts  2.4 us

profile of v3, /device:TPU:1, one launch (start us, length us, event | category | flops | bytes accessed | tf_op | source)
XLA Modules:
  0.0 56.7 jit_solution(10555446713170002748)
XLA Ops:
  0.6 53.6 %shard_map.113 = (bf16[2,5,160,100]{3,2,1,0:T(8,128)(2,1)}, f32[64,128]{1,0:T(8,128)}) custom-call(bf16[1,100,2688]{2,1,0:T(8,128)(2,1)} %phys_hbm.1, bf16[5,128,640]{2,1,0:T(8,128)(2,1)} %poly_hbm.1, bf16[1,21,128,128]{3,2,1,0:T(8,128)(2,1)} %s2a_hbm.1, bf16[4,2,128,128]{3,2,1,0:T(8,128)(2,1)} %a2s_hbm.1, f32[64,128]{1,0:T(8,128)} %bitcast.7, ...), custom_call_target="tpu_custom_call" | custom-call | flops 1000000000 | bytes 3000000 | tf_op jit(solution)/shard_map/pallas_call | solution.py:843
  54.2 0.0 copy-start
  54.3 1.8 %copy.14 = bf16[100,2,5,160]{0,3,2,1:T(8,128)(2,1)} copy(bf16[100,2,5,160]{0,3,2,1:T(8,128)(2,1)} %bitcast.5) | data formatting | bytes 640000
  56.0 0.0 copy-done
  56.0 0.6 %copy.15 = f32[2,8,4,128]{3,2,1,0:T(4,128)} copy(f32[2,8,4,128]{3,2,1,0:T(4,128)S(1)} %bitcast.6) | data formatting | bytes 65536
Async XLA Ops:
  54.2 1.8 %copy-start = (f32[64,128]{1,0:T(8,128)S(1)}, f32[64,128]{1,0:T(8,128)}, u32[]{:S(2)}) copy-start(f32[64,128]{1,0:T(8,128)} %get-tuple-element.5) | copy-start | bytes 98308

commit v4 on v3

--- a/solution.py
+++ b/solution.py
@@ -104,6 +104,7 @@
     got32,
     product2,
     product0,
+    degrees_all,
     plane32,
     select_y,
     bulk,
@@ -183,7 +184,10 @@
     band = [(x, row, lax.rem(col + i, NCOL)) for i in range(1, NCOL)]
     after = band[0]
     before = band[-1]
-    z_ring = [at(x, y, lax.rem(z + i, NZ), core) for i in range(1, NZ)]
+    z_ring = [
+        at(x, y, lax.rem(z + i, NZ), core)
+        for i in (8, 7, 9, 6, 10, 5, 11, 4, 12, 3, 13, 2, 14, 1, 15)
+    ]
     y_ring = [at(x, lax.rem(y + i, NY), z, core) for i in range(1, NY)]
     x_ring = [at(lax.rem(x + i, NX), y, z, core) for i in range(1, NX)]
     sibling = at(x, y, z, 1 - core)
@@ -459,10 +463,10 @@
     for device in x_ring:
         pl.semaphore_signal(ready2, inc=1, device_id=device, device_id_type=MESH)
 
-    for j in range(NY):
+    def post_group(j):
         yy = lax.rem(y + j, NY)
 
-        def post(i, _, j=j, yy=yy):
+        def post(i, _):
             zz = lax.rem(z + i, NZ)
             remote(
                 outbox.at[zz * NY + yy],
@@ -476,6 +480,9 @@
         lax.fori_loop(1, NZ, post, 0)
         if j:
             post(0, 0)
+
+    post_group(0)
+    post_group(1)
     inbox[0, pl.ds(y, 1), pl.ds(z, 1)] = outbox[pl.ds(z * NY + y, 1)][None]
 
     ins[1].wait()
@@ -564,6 +571,8 @@
         copy.start()
         ring_on.append(copy)
 
+    post_group(2)
+    post_group(3)
     circulate(0)
     circulate(1)
 
@@ -616,6 +625,21 @@
             device,
         )
 
+    pass_on(2)
+    pass_on(3)
+    def unpack(slot):
+        got32[...] = inbox[slot].astype(F32).reshape(CHIPS * 2 * PACKED, SPAN)
+
+        def spread_row(r, _):
+            columns = pl.ds(pl.multiple_of(r * SPAN, SPAN), SPAN)
+            right_hand[slot * LATS : (slot + 1) * LATS, columns] = got32[
+                pl.ds(r, LATS, stride=PACKED), :
+            ].astype(BF16)
+            return 0
+
+        lax.fori_loop(0, PACKED, spread_row, 0)
+
+    unpack(0)
     many(NZ - 1, sibling).wait_recv()
     stretch = plane_got[...].astype(F32).reshape(NZ * 16, SPAN)
     stretch = pltpu.roll(stretch, lax.rem(SPAN - NY * z, SPAN), 1)
@@ -630,8 +654,9 @@
     mixed_send[...] = mixed
     pl.semaphore_wait(ready2, NX - 1)
     mixed_got[pl.ds(y * 2 + core, 1)] = mixed[None]
-    for i in range(1, NX * NY * NCORE):
-        dx, dy, dc = i // 8, (i // 2) % 4, i % 2
+    steps = [(i // 8, (i // 2) % 4, i % 2) for i in range(1, NX * NY * NCORE)]
+    hops = (0, 1, 2, 1)
+    for dx, dy, dc in sorted(steps, key=lambda t: -hops[t[0]] - hops[t[1]]):
         cc = 1 - core if dc else core
         remote(
             mixed_send,
@@ -641,16 +666,6 @@
             at(lax.rem(x + dx, NX), lax.rem(y + dy, NY), z, cc),
         ).start()
 
-    def unpack(slot):
-        got32[...] = inbox[slot].astype(F32).reshape(CHIPS * 2 * PACKED, SPAN)
-        for r in range(PACKED):
-            right_hand[slot * LATS : (slot + 1) * LATS, r * SPAN : (r + 1) * SPAN] = got32[
-                pl.ds(r, LATS, stride=PACKED), :
-            ].astype(BF16)
-
-    unpack(0)
-    pass_on(2)
-    pass_on(3)
     unpack(1)
     unpack(3)
     for copy in poly_copies:
@@ -660,12 +675,16 @@
         copy.wait_recv()
     unpack(2)
 
-    for c in range(2):
-        for pair in range(2):
-            start = (c * PARTS + pair * 2) * SPAN
-            product2[:, start : start + 2 * SPAN] = jnp.dot(
-                degrees, right_hand[:, start : start + 2 * SPAN], preferred_element_type=F32
-            )
+    degrees_all[...] = degrees
+
+    def legendre(i, _):
+        columns = pl.ds(pl.multiple_of(i * 2 * SPAN, 2 * SPAN), 2 * SPAN)
+        product2[:, columns] = jnp.dot(
+            degrees_all[...], right_hand[:, columns], preferred_element_type=F32
+        )
+        return 0
+
+    lax.fori_loop(0, 4, legendre, 0)
     lanes = lax.broadcasted_iota(jnp.int32, (DEGREES, SPAN), 1)
     for c in range(2):
         for k in range(WAVES):
@@ -785,6 +804,7 @@
         pltpu.VMEM((LATS * PACKED, SPAN), F32),
         pltpu.VMEM((WAVES * DEGREES, PACKED * SPAN), F32),
         pltpu.VMEM((WAVES * DEGREES, SPAN), F32),
+        pltpu.VMEM((WAVES * DEGREES, NX * LATS), BF16),
         pltpu.VMEM((16, SPAN), F32),
         pltpu.VMEM((8 * SPAN, SPAN), BF16),
         pltpu.VMEM((2, WAVES, DEGREES, SPAN), F32),

time: 56.8 us -> 57.2 us (level); the launches traced: 56.7 us -> 56.1 us
  Pallas kernels: 53.6 us -> 53 us
    pallas_call x1, Pallas kernels: 53.6 us -> 53 us  [local(): pl.pallas_call(kernel, out_shape=(jax.ShapeDtypeStruct((2, WAVES, DEGREES...]
where the time goes in v4:
time: 57.2 us; the launch traced here: 56.1 us
  Pallas kernels  53 us (93%)
  local copies, waits for them, and re-layouts  2.4 us (4%)
  between operations  0.65 us (1%)
    pallas_call x1, Pallas kernels, local(): pl.pallas_call(kernel, out_shape=(jax.ShapeDtypeStruct((2, WAVES, DEGREES...  53 us
    unnamed x4, local copies, waits for them, and re-layouts  2.4 us

profile of v4, /device:TPU:1, one launch (start us, length us, event | category | flops | bytes accessed | tf_op | source)
XLA Modules:
  0.0 56.1 jit_solution(3941298047954704606)
XLA Ops:
  0.6 53.0 %shard_map.113 = (bf16[2,5,160,100]{3,2,1,0:T(8,128)(2,1)}, f32[64,128]{1,0:T(8,128)}) custom-call(bf16[1,100,2688]{2,1,0:T(8,128)(2,1)} %phys_hbm.1, bf16[5,128,640]{2,1,0:T(8,128)(2,1)} %poly_hbm.1, bf16[1,21,128,128]{3,2,1,0:T(8,128)(2,1)} %s2a_hbm.1, bf16[4,2,128,128]{3,2,1,0:T(8,128)(2,1)} %a2s_hbm.1, f32[64,128]{1,0:T(8,128)} %bitcast.7, ...), custom_call_target="tpu_custom_call" | custom-call | flops 1000000000 | bytes 3000000 | tf_op jit(solution)/shard_map/pallas_call | solution.py:863
  53.6 0.0 copy-start
  53.7 1.8 %copy.14 = bf16[100,2,5,160]{0,3,2,1:T(8,128)(2,1)} copy(bf16[100,2,5,160]{0,3,2,1:T(8,128)(2,1)} %bitcast.5) | data formatting | bytes 640000
  55.4 0.0 copy-done
  55.4 0.6 %copy.15 = f32[2,8,4,128]{3,2,1,0:T(4,128)} copy(f32[2,8,4,128]{3,2,1,0:T(4,128)S(1)} %bitcast.6) | data formatting | bytes 65536
Async XLA Ops:
  53.6 1.8 %copy-start = (f32[64,128]{1,0:T(8,128)S(1)}, f32[64,128]{1,0:T(8,128)}, u32[]{:S(2)}) copy-start(f32[64,128]{1,0:T(8,128)} %get-tuple-element.5) | copy-start | bytes 98308

commit v5 on v4

--- a/solution.py
+++ b/solution.py
@@ -463,10 +463,10 @@
     for device in x_ring:
         pl.semaphore_signal(ready2, inc=1, device_id=device, device_id_type=MESH)
 
-    def post_group(j):
+    for j in range(NY):
         yy = lax.rem(y + j, NY)
 
-        def post(i, _):
+        def post(i, _, j=j, yy=yy):
             zz = lax.rem(z + i, NZ)
             remote(
                 outbox.at[zz * NY + yy],
@@ -480,9 +480,6 @@
         lax.fori_loop(1, NZ, post, 0)
         if j:
             post(0, 0)
-
-    post_group(0)
-    post_group(1)
     inbox[0, pl.ds(y, 1), pl.ds(z, 1)] = outbox[pl.ds(z * NY + y, 1)][None]
 
     ins[1].wait()
@@ -571,8 +568,6 @@
         copy.start()
         ring_on.append(copy)
 
-    post_group(2)
-    post_group(3)
     circulate(0)
     circulate(1)
 

time: 57.2 us -> 56.4 us (0.986); the launches traced: 56.1 us -> 56.2 us
  no operation moved by 1% of the time
where the time goes in v5:
time: 56.4 us; the launch traced here: 56.2 us
  Pallas kernels  53.2 us (94%)
  local copies, waits for them, and re-layouts  2.4 us (4%)
  between operations  0.65 us (1%)
    pallas_call x1, Pallas kernels, local(): pl.pallas_call(kernel, out_shape=(jax.ShapeDtypeStruct((2, WAVES, DEGREES...  53.2 us
    unnamed x4, local copies, waits for them, and re-layouts  2.4 us

profile of v5, /device:TPU:1, one launch (start us, length us, event | category | flops | bytes accessed | tf_op | source)
XLA Modules:
  0.0 56.2 jit_solution(17968110737500404061)
XLA Ops:
  0.6 53.2 %shard_map.113 = (bf16[2,5,160,100]{3,2,1,0:T(8,128)(2,1)}, f32[64,128]{1,0:T(8,128)}) custom-call(bf16[1,100,2688]{2,1,0:T(8,128)(2,1)} %phys_hbm.1, bf16[5,128,640]{2,1,0:T(8,128)(2,1)} %poly_hbm.1, bf16[1,21,128,128]{3,2,1,0:T(8,128)(2,1)} %s2a_hbm.1, bf16[4,2,128,128]{3,2,1,0:T(8,128)(2,1)} %a2s_hbm.1, f32[64,128]{1,0:T(8,128)} %bitcast.7, ...), custom_call_target="tpu_custom_call" | custom-call | flops 1000000000 | bytes 3000000 | tf_op jit(solution)/shard_map/pallas_call | solution.py:858
  53.8 0.0 copy-start
  53.8 1.8 %copy.14 = bf16[100,2,5,160]{0,3,2,1:T(8,128)(2,1)} copy(bf16[100,2,5,160]{0,3,2,1:T(8,128)(2,1)} %bitcast.5) | data formatting | bytes 640000
  55.6 0.0 copy-done
  55.6 0.6 %copy.15 = f32[2,8,4,128]{3,2,1,0:T(4,128)} copy(f32[2,8,4,128]{3,2,1,0:T(4,128)S(1)} %bitcast.6) | data formatting | bytes 65536
Async XLA Ops:
  53.8 1.8 %copy-start = (f32[64,128]{1,0:T(8,128)S(1)}, f32[64,128]{1,0:T(8,128)}, u32[]{:S(2)}) copy-start(f32[64,128]{1,0:T(8,128)} %get-tuple-element.5) | copy-start | bytes 98308

commit v6 on v5

--- a/solution.py
+++ b/solution.py
@@ -622,12 +622,16 @@
 
     pass_on(2)
     pass_on(3)
+    order = (0, 1, 3, 2)
+    early = 3 * LATS
+
     def unpack(slot):
+        place = order.index(slot)
         got32[...] = inbox[slot].astype(F32).reshape(CHIPS * 2 * PACKED, SPAN)
 
         def spread_row(r, _):
             columns = pl.ds(pl.multiple_of(r * SPAN, SPAN), SPAN)
-            right_hand[slot * LATS : (slot + 1) * LATS, columns] = got32[
+            right_hand[place * LATS : (place + 1) * LATS, columns] = got32[
                 pl.ds(r, LATS, stride=PACKED), :
             ].astype(BF16)
             return 0
@@ -665,21 +669,29 @@
     unpack(3)
     for copy in poly_copies:
         copy.wait_recv()
-    degrees = jnp.concatenate([poly_got[i] for i in range(NX)], axis=1)
+    degrees = jnp.concatenate([poly_got[i] for i in order], axis=1)
+    degrees_all[...] = degrees
+
+    def legendre(i, _):
+        columns = pl.ds(pl.multiple_of(i * 2 * SPAN, 2 * SPAN), 2 * SPAN)
+        product2[:, columns] = jnp.dot(
+            degrees_all[:, :early], right_hand[:early, columns], preferred_element_type=F32
+        )
+        return 0
+
+    lax.fori_loop(0, 4, legendre, 0)
     for copy in ring_on:
         copy.wait_recv()
     unpack(2)
 
-    degrees_all[...] = degrees
-
-    def legendre(i, _):
+    def legendre_last(i, _):
         columns = pl.ds(pl.multiple_of(i * 2 * SPAN, 2 * SPAN), 2 * SPAN)
-        product2[:, columns] = jnp.dot(
-            degrees_all[...], right_hand[:, columns], preferred_element_type=F32
+        product2[:, columns] += jnp.dot(
+            degrees_all[:, early:], right_hand[early:, columns], preferred_element_type=F32
         )
         return 0
 
-    lax.fori_loop(0, 4, legendre, 0)
+    lax.fori_loop(0, 4, legendre_last, 0)
     lanes = lax.broadcasted_iota(jnp.int32, (DEGREES, SPAN), 1)
     for c in range(2):
         for k in range(WAVES):
@@ -706,7 +718,7 @@
     )
     sorted_rows = jnp.dot(stacked, select_y[...], preferred_element_type=F32).astype(BF16)
     surface_rows = jnp.concatenate(
-        [sorted_rows[slot * 16 : (slot + 1) * 16, :] for slot in range(NX)], axis=1
+        [sorted_rows[slot * 16 : (slot + 1) * 16, :] for slot in order], axis=1
     )
     surface_rows = jnp.concatenate(
         [surface_rows, jnp.zeros((SPAN - 16, NX * LATS), BF16)], axis=0

time: 56.4 us -> 56.4 us (level)
  no operation moved by 1% of the time
where the time goes in v6:
time: 56.4 us; the launch traced here: 56.2 us
  Pallas kernels  53.2 us (94%)
  local copies, waits for them, and re-layouts  2.4 us (4%)
  between operations  0.65 us (1%)
    pallas_call x1, Pallas kernels, local(): pl.pallas_call(kernel, out_shape=(jax.ShapeDtypeStruct((2, WAVES, DEGREES...  53.2 us
    unnamed x4, local copies, waits for them, and re-layouts  2.4 us

profile of v6, /device:TPU:1, one launch (start us, length us, event | category | flops | bytes accessed | tf_op | source)
XLA Modules:
  0.0 56.2 jit_solution(1152622754955385663)
XLA Ops:
  0.6 53.2 %shard_map.113 = (bf16[2,5,160,100]{3,2,1,0:T(8,128)(2,1)}, f32[64,128]{1,0:T(8,128)}) custom-call(bf16[1,100,2688]{2,1,0:T(8,128)(2,1)} %phys_hbm.1, bf16[5,128,640]{2,1,0:T(8,128)(2,1)} %poly_hbm.1, bf16[1,21,128,128]{3,2,1,0:T(8,128)(2,1)} %s2a_hbm.1, bf16[4,2,128,128]{3,2,1,0:T(8,128)(2,1)} %a2s_hbm.1, f32[64,128]{1,0:T(8,128)} %bitcast.7, ...), custom_call_target="tpu_custom_call" | custom-call | flops 1000000000 | bytes 3000000 | tf_op jit(solution)/shard_map/pallas_call | solution.py:870
  53.8 0.0 copy-start
  53.8 1.8 %copy.14 = bf16[100,2,5,160]{0,3,2,1:T(8,128)(2,1)} copy(bf16[100,2,5,160]{0,3,2,1:T(8,128)(2,1)} %bitcast.5) | data formatting | bytes 640000
  55.6 0.0 copy-done
  55.6 0.6 %copy.15 = f32[2,8,4,128]{3,2,1,0:T(4,128)} copy(f32[2,8,4,128]{3,2,1,0:T(4,128)S(1)} %bitcast.6) | data formatting | bytes 65536
Async XLA Ops:
  53.8 1.8 %copy-start = (f32[64,128]{1,0:T(8,128)S(1)}, f32[64,128]{1,0:T(8,128)}, u32[]{:S(2)}) copy-start(f32[64,128]{1,0:T(8,128)} %get-tuple-element.5) | copy-start | bytes 98308
